TPU v7x, 128 devices: a whole 4x4x4 slice. The times are simulated.
128 devices in a mesh: section: 2 (over core), block: 64 (over x, z, y).
Axes of the slice: x: 4, y: 4, z: 4, core: 2. Of those that a mesh axis runs over, the one named last changes fastest.
Arguments:
- state: float32 [2, 64, 5, 32, 1024], P('section', 'block'), may hold values from -1 to 3.5, as said below
- mean_flow: float32 [64, 5, 32, 1024], P('block'), may hold values from -0.5 to 1.5, as said below
- les_owner: int32 [64], replicated, may hold values from 0 to 63, each once
- ac_owner: int32 [64], replicated, may hold values from 0 to 63, each once
- les_nbr: int32 [64, 6], replicated, may hold values from -1 to 63, as said below
- ac_nbr: int32 [64, 6], replicated, may hold values from -1 to 63, as said below
- coupling: int32 [64], replicated, may hold values from 0 to 63, each once
Outputs:
- advanced: float32 [2, 64, 5, 32, 1024], P('section', 'block')
Inputs may be any that keep to these rules, and one draw needn't show every extreme that they name: `state`: section 0: density 1 to 1.5, momenta -0.4 to 0.4, pressure 0.4 (E - m.m / (2 r)) 0.7 to 1.3. Section 1: all entries -1 to 1. `mean_flow`: mean density 0.8 to 1.5, mean velocities -0.5 to 0.5, mean pressure 0.7 to 1.3. `les_nbr`: blocks sit on a 4 x 4 x 64/16 grid of equal blocks; an entry names the block beside it across that face, and that block names it back across the opposite face. `ac_nbr`: blocks sit on a 4 x 4 x 64/16 grid of equal blocks; an entry names the block beside it across that face, and that block names it back across the opposite face.
All inputs are finite; a program needn't handle non-finite values.
Results may differ from a plain program's by a relative error of at most 0.0003.
Values may be sent and summed in bfloat16 or wider, within the bound.
A program may use at most 128 MiB of HBM per device.

v0:
```python
import jax
import jax.numpy as jnp
from jax import lax
from jax.sharding import Mesh
from jax.sharding import PartitionSpec as P

STEPS = 2
BLOCK = ("block_0", "block_1", "block_2")


GAMMA_LESS = 0.4
DT_LES = 0.2
DT_AC = 0.3
VISCOSITY = 0.05
FEEDBACK_GAIN = 0.5


def as_sent(array):
    return jax.tree.map(lambda a: a.astype(jnp.bfloat16) if a.dtype == jnp.float32 else a, array)


def cut_along(array, dim, devices):
    before, after = (array.shape[:dim], array.shape[dim + 1 :])
    return jnp.moveaxis(array.reshape(*before, devices, -1, *after), dim, 0)


def joined_along(blocks, dim):
    blocks = jnp.moveaxis(blocks, 0, dim)
    lengths = blocks.shape
    return blocks.reshape(*lengths[:dim], lengths[dim] * lengths[dim + 1], *lengths[dim + 2 :])


def moved_by_axis(blocks, axes, turns):
    inside = blocks.shape[1:]
    result = blocks.reshape(*(lax.axis_size(a) for a in axes), *inside)
    for k in turns:
        result = lax.all_to_all(result, axes[k], k, k, tiled=True)
    return result.reshape(-1, *inside)


def one_axis_at_a_time(array, axes, turns, split_dim, concat_dim):
    blocks = cut_along(array, split_dim, lax.axis_size(axes))
    return joined_along(moved_by_axis(blocks, axes, turns), concat_dim)


def partner_2(array, axis, stride):
    return lax.ppermute(array, axis, [(i, i ^ 1 << stride) for i in range(lax.axis_size(axis))])


def face_layers(volume):
    num_blocks, num_vars, cube_side, face_cells = volume.shape
    members = [
        volume[:, :, 0, :],
        volume[:, :, cube_side - 1, :],
        volume[:, :, :, 0:cube_side].reshape(num_blocks, num_vars, face_cells),
        volume[:, :, :, (cube_side - 1) * cube_side :].reshape(num_blocks, num_vars, face_cells),
        volume[:, :, :, 0::cube_side].reshape(num_blocks, num_vars, face_cells),
        volume[:, :, :, cube_side - 1 :: cube_side].reshape(num_blocks, num_vars, face_cells),
    ]
    return jnp.stack(members, axis=1)


def neighbours(volume, halo_cells):
    num_blocks, num_vars, cube_side, face_cells = volume.shape

    def face_grid(direction):
        return halo_cells[:, direction].reshape(num_blocks, num_vars, cube_side, cube_side)

    low_x = jnp.concatenate([halo_cells[:, 0][:, :, None, :], volume[:, :, :-1, :]], axis=2)
    high_x = jnp.concatenate([volume[:, :, 1:, :], halo_cells[:, 1][:, :, None, :]], axis=2)
    low_y = jnp.concatenate([face_grid(2), volume[:, :, :, :-cube_side]], axis=3)
    high_y = jnp.concatenate([volume[:, :, :, cube_side:], face_grid(3)], axis=3)
    z_index = lax.broadcasted_iota(jnp.int32, (1, 1, 1, face_cells), 3) % cube_side
    low_z = jnp.where(
        z_index == 0, jnp.repeat(face_grid(4), cube_side, axis=3), jnp.roll(volume, 1, axis=3)
    )
    high_z = jnp.where(
        z_index == cube_side - 1,
        jnp.repeat(face_grid(5), cube_side, axis=3),
        jnp.roll(volume, -1, axis=3),
    )
    return ((low_x, high_x), (low_y, high_y), (low_z, high_z))


def primitives(conserved):
    density = conserved[:, 0]
    momentum = conserved[:, 1:4]
    energy = conserved[:, 4]
    velocity = momentum / density[:, None]
    pressure = GAMMA_LESS * (energy - 0.5 * jnp.sum(momentum * velocity, axis=1))
    return (momentum, energy, velocity, pressure)


def flux_along(conserved, axis_k):
    momentum, energy, velocity, pressure = primitives(conserved)
    normal_speed = velocity[:, axis_k]
    members = [momentum[:, axis_k]]
    for component in range(3):
        entry_term = momentum[:, component] * normal_speed
        if component == axis_k:
            entry_term = entry_term + pressure
        members.append(entry_term)
    members.append((energy + pressure) * normal_speed)
    return (jnp.stack(members, axis=1), velocity)


def les_both(conserved, halo_cells):
    pairs = neighbours(conserved, halo_cells)
    momentum, energy, velocity, pressure = primitives(conserved)
    flux_sum = jnp.zeros_like(conserved)
    laplace = -6.0 * conserved
    gradient = []
    for axis_k in range(3):
        low_side, high_side = pairs[axis_k]
        flux_low, speed_low = flux_along(low_side, axis_k)
        flux_high, speed_high = flux_along(high_side, axis_k)
        flux_sum = flux_sum + 0.5 * (flux_high - flux_low)
        laplace = laplace + low_side + high_side
        gradient.append(0.5 * (speed_high - speed_low))
    vort_x = gradient[1][:, 2] - gradient[2][:, 1]
    vort_y = gradient[2][:, 0] - gradient[0][:, 2]
    vort_z = gradient[0][:, 1] - gradient[1][:, 0]
    lamb_vector = jnp.stack(
        [
            vort_y * velocity[:, 2] - vort_z * velocity[:, 1],
            vort_z * velocity[:, 0] - vort_x * velocity[:, 2],
            vort_x * velocity[:, 1] - vort_y * velocity[:, 0],
        ],
        axis=1,
    ).astype(jnp.bfloat16)
    updated = conserved + DT_LES * (VISCOSITY * laplace - flux_sum)
    return (updated, lamb_vector)


def resting(conserved, halo_cells):
    return (conserved, conserved[:, 1:4].astype(jnp.bfloat16))


def acoustic_advance(perturb, halo_cells, mean_state, source):
    pairs = neighbours(perturb, halo_cells)
    slopes = [0.5 * (high_side - low_side) for low_side, high_side in pairs]
    mean_density = mean_state[:, 0]
    mean_pressure = mean_state[:, 4]
    carried = (
        mean_state[:, 1][:, None] * slopes[0]
        + mean_state[:, 2][:, None] * slopes[1]
        + mean_state[:, 3][:, None] * slopes[2]
    )
    divergence = slopes[0][:, 1] + slopes[1][:, 2] + slopes[2][:, 3]
    members = [carried[:, 0] + mean_density * divergence]
    for axis_k in range(3):
        members.append(
            carried[:, 1 + axis_k] + slopes[axis_k][:, 4] / mean_density + source[:, axis_k]
        )
    members.append(carried[:, 4] + 1.4 * mean_pressure * divergence)
    return perturb - DT_AC * jnp.stack(members, axis=1)


def keep_les(advanced, halo_cells, mean_state, source):
    return advanced.at[:, 1:4].add(DT_LES * FEEDBACK_GAIN * source.astype(jnp.float32))


def acoustic_branch(advanced, halo_cells, mean_state, source):
    return acoustic_advance(advanced, halo_cells, mean_state, source.astype(jnp.float32))


def lookup_rows(lookup_table, positions):
    count = lookup_table.shape[0]
    matches = (positions[..., None] == lax.broadcasted_iota(jnp.int32, (count,), 0)).astype(
        jnp.int32
    )
    flat_table = lookup_table.reshape(count, -1)
    picked = jnp.sum(matches[..., None] * flat_table, axis=-2)
    return picked.reshape(positions.shape + lookup_table.shape[1:])


def invert(owner_list):
    count = owner_list.shape[0]
    slots = lax.broadcasted_iota(jnp.int32, (count, count), 0)
    blocks = lax.broadcasted_iota(jnp.int32, (count, count), 1)
    matches = (owner_list[None, :] == slots).astype(jnp.int32)
    return jnp.sum(matches * blocks, axis=1)


def on_device(state, mean_flow, les_owner, ac_owner, les_nbr, ac_nbr, coupling):
    section = lax.axis_index("section")
    device = lax.axis_index(BLOCK)
    devices = lax.axis_size(BLOCK)
    local_state = state[0]
    per_dev = local_state.shape[0]
    total_blocks = per_dev * devices
    les_side = section == 0
    owner_list = jnp.where(les_side, les_owner, ac_owner)
    partner_table = jnp.where(les_side, les_nbr, ac_nbr)
    inverse = invert(owner_list)
    partner = lookup_rows(partner_table, inverse)
    present = partner >= 0
    source_slot = lookup_rows(owner_list, jnp.maximum(partner, 0))
    opposite = jnp.bitwise_xor(lax.broadcasted_iota(jnp.int32, (1, 6), 1), 1)
    wanted = source_slot * 6 + opposite
    start_row = device * per_dev
    own_present = lax.dynamic_slice_in_dim(present, start_row, per_dev, 0)
    coupled = lookup_rows(les_owner, lookup_rows(coupling, invert(ac_owner)))
    feed_slot = lookup_rows(ac_owner, lookup_rows(invert(coupling), invert(les_owner)))
    pairing = jnp.where(les_side, feed_slot, coupled)
    current = local_state
    for step_index in range(STEPS):
        face_cells = face_layers(current)
        pieces = lax.all_to_all(
            as_sent(face_cells), BLOCK, split_axis=3, concat_axis=0, tiled=True
        ).astype(face_cells.dtype)
        flattened = pieces.reshape((total_blocks * 6,) + pieces.shape[2:])
        chosen = jnp.take(flattened, wanted.reshape(-1), axis=0).reshape(
            (total_blocks, 6) + pieces.shape[2:]
        )
        arrived = lax.all_to_all(
            as_sent(chosen), BLOCK, split_axis=0, concat_axis=3, tiled=True
        ).astype(chosen.dtype)
        halo_cells = jnp.where(own_present[:, :, None, None], arrived, face_cells)
        advanced, outgoing = lax.cond(les_side, les_both, resting, current, halo_cells)
        spread = one_axis_at_a_time(outgoing.reshape(per_dev, 3, -1), BLOCK, (0, 1, 2), 2, 0)
        crossed = partner_2(spread, "section", 0)
        ordered = jnp.take(crossed, pairing, axis=0)
        source = lax.all_to_all(ordered, BLOCK, split_axis=0, concat_axis=2, tiled=True).reshape(
            outgoing.shape
        )
        current = lax.cond(
            les_side, keep_les, acoustic_branch, advanced, halo_cells, mean_flow, source
        )
    return current[None]


def solution(mesh):
    finer = Mesh(
        mesh.devices.reshape(mesh.shape["section"], 4, 4, 4),
        ("section", "block_0", "block_1", "block_2"),
    )
    placed = (
        P("section", BLOCK, None, None, None),
        P(BLOCK, None, None, None),
        P(),
        P(),
        P(),
        P(),
        P(),
    )
    return jax.shard_map(
        on_device,
        mesh=finer,
        in_specs=placed,
        out_specs=P("section", BLOCK, None, None, None),
        check_vma=False,
    )
```

profile of v0, /device:TPU:1, one launch (start us, length us, event | category | flops | bytes accessed | tf_op | source)
XLA Modules:
  0.0 272.5 jit_solution(16377075570456173898)
XLA Ops:
  0.0 1.5 squeeze.37
  2.1 2.1 slice.762
  4.1 2.1 slice.763
  9.1 1.5 copy.187
  10.6 3.4 %reshape.3572 = bf16[64,2,240]{2,1,0:T(2,128)(2,1)} reshape(bf16[1024,1,6,5]{3,2,1,0:T(8,128)(2,1)S(1)} %bitcast.268) | data formatting | bytes 122880
  14.0 12.3 %all-to-all-start = ((bf16[64,2,240]{2,1,0:T(2,128)(2,1)}), bf16[64,2,240]{2,1,0:T(2,128)(2,1)S(1)}, u32[]{:S(2)}, u32[]{:S(2)}) async-start(bf16[64,2,240]{2,1,0:T(2,128)(2,1)} %reshape.3572), calls=%async_computation | async-start | bytes 131072 | tf_op jit(solution)/shard_map/all_to_all | solution.py:209
  27.4 7.4 %all-to-all-done = bf16[64,2,240]{2,1,0:T(2,128)(2,1)S(1)} async-done(((bf16[64,2,240]{2,1,0:T(2,128)(2,1)}), bf16[64,2,240]{2,1,0:T(2,128)(2,1)S(1)}, u32[]{:S(2)}, u32[]{:S(2)}) %all-to-all-start) | async-done | bytes 61472 | tf_op jit(solution)/shard_map/all_to_all | solution.py:209
  34.8 3.6 %reshape.3573 = bf16[1024,1,6,5]{3,2,1,0:T(8,128)(2,1)S(1)} reshape(bf16[64,2,240]{2,1,0:T(2,128)(2,1)S(1)} %all-to-all-done) | data formatting | bytes 122880
  38.4 1.6 copy.188
  41.1 1.7 gather_fusion
  43.2 2.9 %reshape.3525 = bf16[64,6,5,16]{1,0,3,2:T(8,128)(2,1)S(1)} reshape(bf16[384,5,16]{0,2,1:T(8,128)(2,1)S(1)} %select_convert_fusion.1) | data formatting | bytes 122880 | tf_op jit(solution)/shard_map/convert_element_type | solution.py:19
  46.1 2.9 %copy.193 = bf16[64,6,5,16]{3,1,2,0:T(8,128)(2,1)S(1)} copy(bf16[64,6,5,16]{1,0,3,2:T(8,128)(2,1)S(1)} %reshape.3525) | data formatting | bytes 122880 | tf_op jit(solution)/shard_map/convert_element_type | solution.py:19
  49.0 1.1 reshape.3574
  50.1 5.0 %all-to-all-start.1 = ((bf16[64,2,240]{2,1,0:T(2,128)(2,1)}), bf16[64,2,240]{2,1,0:T(2,128)(2,1)S(1)}, u32[]{:S(2)}, u32[]{:S(2)}) async-start(bf16[64,2,240]{2,1,0:T(2,128)(2,1)} %reshape.3574), calls=%async_computation.1 | async-start | bytes 131072 | tf_op jit(solution)/shard_map/all_to_all | solution.py:216
  55.3 8.2 %all-to-all-done.1 = bf16[64,2,240]{2,1,0:T(2,128)(2,1)S(1)} async-done(((bf16[64,2,240]{2,1,0:T(2,128)(2,1)}), bf16[64,2,240]{2,1,0:T(2,128)(2,1)S(1)}, u32[]{:S(2)}, u32[]{:S(2)}) %all-to-all-start.1) | async-done | bytes 61472 | tf_op jit(solution)/shard_map/all_to_all | solution.py:216
  64.6 0.9 broadcast_select_fusion.3
  65.5 1.3 conditional.6
  66.9 1.0 reshape_reshape.12
  68.7 3.4 %all-to-all-start.2 = ((bf16[4,4,4,1,3,512]{5,2,4,3,1,0:T(4,128)(2,1)}), bf16[4,4,4,1,3,512]{5,2,4,3,1,0:T(4,128)(2,1)S(1)}, u32[]{:S(2)}, u32[]{:S(2)}) async-start(bf16[4,4,4,1,3,512]{5,2,4,3,1,0:T(4,128)(2,1)} %copy.197), calls=%async_computation.2 | async-start | bytes 393216 | tf_op jit(solution)/shard_map/all_to_all | solution.py:37
  73.0 4.2 %all-to-all-done.2 = bf16[4,4,4,1,3,512]{5,2,4,3,1,0:T(4,128)(2,1)S(1)} async-done(((bf16[4,4,4,1,3,512]{5,2,4,3,1,0:T(4,128)(2,1)}), bf16[4,4,4,1,3,512]{5,2,4,3,1,0:T(4,128)(2,1)S(1)}, u32[]{:S(2)}, u32[]{:S(2)}) %all-to-all-start.2) | async-done | bytes 196640 | tf_op jit(solution)/shard_map/all_to_all | solution.py:37
  77.9 3.4 %all-to-all-start.3 = ((bf16[4,4,4,1,3,512]{5,2,4,3,0,1:T(4,128)(2,1)}), bf16[4,4,4,1,3,512]{5,2,4,3,0,1:T(4,128)(2,1)S(1)}, u32[]{:S(2)}, u32[]{:S(2)}) async-start(bf16[4,4,4,1,3,512]{5,2,4,3,0,1:T(4,128)(2,1)} %copy.198), calls=%async_computation.3 | async-start | bytes 393216 | tf_op jit(solution)/shard_map/all_to_all | solution.py:37
  81.6 4.8 %all-to-all-done.3 = bf16[4,4,4,1,3,512]{5,2,4,3,0,1:T(4,128)(2,1)S(1)} async-done(((bf16[4,4,4,1,3,512]{5,2,4,3,0,1:T(4,128)(2,1)}), bf16[4,4,4,1,3,512]{5,2,4,3,0,1:T(4,128)(2,1)S(1)}, u32[]{:S(2)}, u32[]{:S(2)}) %all-to-all-start.3) | async-done | bytes 196640 | tf_op jit(solution)/shard_map/all_to_all | solution.py:37
  87.3 3.4 %all-to-all-start.4 = ((bf16[4,4,4,1,3,512]{5,1,4,3,0,2:T(4,128)(2,1)}), bf16[4,4,4,1,3,512]{5,1,4,3,0,2:T(4,128)(2,1)S(1)}, u32[]{:S(2)}, u32[]{:S(2)}) async-start(bf16[4,4,4,1,3,512]{5,1,4,3,0,2:T(4,128)(2,1)} %copy.199), calls=%async_computation.4 | async-start | bytes 393216 | tf_op jit(solution)/shard_map/all_to_all | solution.py:37
  91.0 4.8 %all-to-all-done.4 = bf16[4,4,4,1,3,512]{5,1,4,3,0,2:T(4,128)(2,1)S(1)} async-done(((bf16[4,4,4,1,3,512]{5,1,4,3,0,2:T(4,128)(2,1)}), bf16[4,4,4,1,3,512]{5,1,4,3,0,2:T(4,128)(2,1)S(1)}, u32[]{:S(2)}, u32[]{:S(2)}) %all-to-all-start.4) | async-done | bytes 196640 | tf_op jit(solution)/shard_map/all_to_all | solution.py:37
  95.9 24.1 %collective-permute-start = (bf16[64,3,512]{2,1,0:T(4,128)(2,1)S(1)}, bf16[64,3,512]{2,1,0:T(4,128)(2,1)S(1)}, u32[]{:S(2)}, u32[]{:S(2)}) collective-permute-start(bf16[64,3,512]{2,1,0:T(4,128)(2,1)S(1)} %bitcast.282), channel_id=1, source_target_pairs={{0,64},{64,0},{1,65},{65,1},{2,66},{66,2},{3,67},{67,3},{4,68},{68... | collective-permute-start | bytes 589832 | tf_op jit(solution)/shard_map/ppermute | solution.py:47
  120.1 1.1 collective-permute-done
  122.2 13.5 %all_to_all.96 = bf16[64,3,512]{2,1,0:T(4,128)(2,1)S(1)} all-to-all(bf16[64,3,512]{2,1,0:T(4,128)(2,1)S(1)} %broadcast_select_fusion.1), channel_id=1, replica_groups=mesh['section'=2,'block_0'=4,'block_1'=4,'block_2'=4] {'block_0','block_..., dimensions={0} | all-to-all | bytes 393216 | tf_op jit(solution)/shard_map/all_to_all | solution.py:224
  135.9 20.2 %conditional.7 = (f32[1,5,32,1024]{3,2,1,0:T(8,128)S(1)}) conditional(s32[]{:T(128)} %convert_element_type.153, (f32[1,5,32,1024]{3,2,1,0:T(8,128)S(1)}, f32[1,6,5,1024]{3,0,2,1:T(1,128)}, f32[1,5,32,1024]{3,2,1,0:T(8,128)}, bf16[1,3,32,1024]{3,2,1,0:T(8,128)(2,1)S(1)}) %tuple.52, (f32[1,5,32,1024]{3,2,1,0:T(8,128)S(1)}, ...), branch_computations={%region_18.21_spmd, %region_19.22_spmd} | conditional | flops 4726783 | bytes 37875916 | solution.py:227
  136.1 1.3 fusion.173
  137.3 2.2 slice_reduce_fusion.7
  141.0 1.6 broadcast_in_dim.127
  142.6 2.0 broadcast_in_dim.128
  144.7 1.3 fusion.175
  148.0 1.6 broadcast_in_dim.124
  149.6 2.0 broadcast_in_dim.125
  151.7 2.1 broadcast_multiply_fusion
  154.0 0.9 copy-done.2
  158.3 1.5 copy.204
  159.8 2.8 %reshape.3576 = bf16[64,2,240]{2,1,0:T(2,128)(2,1)S(1)} reshape(bf16[1024,1,6,5]{3,2,1,0:T(8,128)(2,1)S(1)} %bitcast.270) | data formatting | bytes 122880
  162.6 13.7 %all_to_all.97 = bf16[64,2,240]{2,1,0:T(2,128)(2,1)S(1)} all-to-all(bf16[64,2,240]{2,1,0:T(2,128)(2,1)S(1)} %reshape.3576), channel_id=1, replica_groups=mesh['section'=2,'block_0'=4,'block_1'=4,'block_2'=4] {'block_0','block_..., dimensions={0} | all-to-all | bytes 122880 | tf_op jit(solution)/shard_map/all_to_all | solution.py:209
  176.3 3.6 %reshape.3577 = bf16[1024,1,6,5]{3,2,1,0:T(8,128)(2,1)S(1)} reshape(bf16[64,2,240]{2,1,0:T(2,128)(2,1)S(1)} %all_to_all.97) | data formatting | bytes 122880
  179.9 1.6 copy.205
  182.6 1.7 gather_fusion.2
  184.8 2.9 %reshape.3526 = bf16[64,6,5,16]{1,0,3,2:T(8,128)(2,1)S(1)} reshape(bf16[384,5,16]{0,2,1:T(8,128)(2,1)S(1)} %select_convert_fusion) | data formatting | bytes 122880 | tf_op jit(solution)/shard_map/convert_element_type | solution.py:19
  187.7 2.9 %copy.210 = bf16[64,6,5,16]{3,1,2,0:T(8,128)(2,1)S(1)} copy(bf16[64,6,5,16]{1,0,3,2:T(8,128)(2,1)S(1)} %reshape.3526) | data formatting | bytes 122880 | tf_op jit(solution)/shard_map/convert_element_type | solution.py:19
  191.1 13.0 %all_to_all.98 = bf16[64,2,240]{2,1,0:T(2,128)(2,1)S(1)} all-to-all(bf16[64,2,240]{2,1,0:T(2,128)(2,1)S(1)} %reshape.3578), channel_id=1, replica_groups=mesh['section'=2,'block_0'=4,'block_1'=4,'block_2'=4] {'block_0','block_..., dimensions={0} | all-to-all | bytes 122880 | tf_op jit(solution)/shard_map/all_to_all | solution.py:216
  206.7 7.5 %all_to_all.99 = bf16[4,4,4,1,3,512]{5,2,4,3,1,0:T(4,128)(2,1)S(1)} all-to-all(bf16[4,4,4,1,3,512]{5,2,4,3,1,0:T(4,128)(2,1)S(1)} %copy.212), channel_id=1, replica_groups=mesh['section'=2,'block_0'=4,'block_1'=4,'block_2'=4] {'block_0'}, dimensions={0} | all-to-all | bytes 393216 | tf_op jit(solution)/shard_map/all_to_all | solution.py:37
  214.3 7.5 %all_to_all.100 = bf16[4,4,4,1,3,512]{5,2,4,3,0,1:T(4,128)(2,1)S(1)} all-to-all(bf16[4,4,4,1,3,512]{5,2,4,3,0,1:T(4,128)(2,1)S(1)} %copy.213), channel_id=1, replica_groups=mesh['section'=2,'block_0'=4,'block_1'=4,'block_2'=4] {'block_1'}, dimensions={1} | all-to-all | bytes 393216 | tf_op jit(solution)/shard_map/all_to_all | solution.py:37
  222.0 7.5 %all_to_all.101 = bf16[4,4,4,1,3,512]{5,1,4,3,0,2:T(4,128)(2,1)S(1)} all-to-all(bf16[4,4,4,1,3,512]{5,1,4,3,0,2:T(4,128)(2,1)S(1)} %copy.214), channel_id=1, replica_groups=mesh['section'=2,'block_0'=4,'block_1'=4,'block_2'=4] {'block_2'}, dimensions={2} | all-to-all | bytes 393216 | tf_op jit(solution)/shard_map/all_to_all | solution.py:37
  229.7 5.7 %collective-permute-start.1 = (bf16[64,3,512]{2,1,0:T(4,128)(2,1)S(1)}, bf16[64,3,512]{2,1,0:T(4,128)(2,1)S(1)}, u32[]{:S(2)}, u32[]{:S(2)}) collective-permute-start(bf16[64,3,512]{2,1,0:T(4,128)(2,1)S(1)} %bitcast.283), channel_id=1, source_target_pairs={{0,64},{64,0},{1,65},{65,1},{2,66},{66,2},{3,67},{67,3},{4,68},{68... | collective-permute-start | bytes 589832 | tf_op jit(solution)/shard_map/ppermute | solution.py:47
  235.4 1.2 collective-permute-done.1
  236.6 0.9 gather_fusion.3
  237.7 13.5 %all_to_all.102 = bf16[64,3,512]{2,1,0:T(4,128)(2,1)S(1)} all-to-all(bf16[64,3,512]{2,1,0:T(4,128)(2,1)S(1)} %broadcast_select_fusion), channel_id=1, replica_groups=mesh['section'=2,'block_0'=4,'block_1'=4,'block_2'=4] {'block_0','block_..., dimensions={0} | all-to-all | bytes 393216 | tf_op jit(solution)/shard_map/all_to_all | solution.py:224
  251.4 20.9 %conditional.17 = (f32[1,1,5,32,1024]{4,3,2,1,0:T(8,128)}) conditional(s32[]{:T(128)} %convert_element_type.153, (f32[1,5,32,1024]{3,2,1,0:T(8,128)S(1)}, f32[1,6,5,1024]{3,0,2,1:T(1,128)}, f32[1,5,32,1024]{3,2,1,0:T(8,128)}, bf16[1,3,32,1024]{3,2,1,0:T(8,128)(2,1)S(1)}) %tuple.55, (f32[1,5,32,1024]{3,2,1,0:T(8,128)S(1)}, ...), branch_computations={%region_28.31_spmd, %region_29.32_spmd} | conditional | flops 4726783 | bytes 37875916 | solution.py:227
  251.6 1.3 fusion.181
  252.8 2.2 slice_reduce_fusion.15
  256.5 1.6 broadcast_in_dim.139
  258.1 2.0 broadcast_in_dim.140
  260.2 1.3 fusion.183
  263.5 1.6 broadcast_in_dim.136
  265.1 2.0 broadcast_in_dim.137
  267.1 2.1 broadcast_multiply_fusion.3
  269.5 0.9 copy-done.4
  271.4 0.9 subtract_bitcast_fusion
  (184 shorter events, 30.0 us)
Async XLA Ops:
  9.0 17.2 %copy-start.28 = (s32[64]{0:T(128)S(1)}, s32[64]{0:T(128)}, u32[]{:S(2)}) copy-start(s32[64]{0:T(128)} %param.25) | copy-start | bytes 772
  9.0 17.2 %copy-start.29 = (s32[64]{0:T(128)S(1)}, s32[64]{0:T(128)}, u32[]{:S(2)}) copy-start(s32[64]{0:T(128)} %param.26) | copy-start | bytes 772
  9.1 17.4 %copy-start.26 = (s32[64,6]{0,1:T(8,128)S(1)}, s32[64,6]{0,1:T(8,128)}, u32[]{:S(2)}) copy-start(s32[64,6]{0,1:T(8,128)} %param.27) | copy-start | bytes 4612
  9.1 17.4 %copy-start.27 = (s32[64,6]{0,1:T(8,128)S(1)}, s32[64,6]{0,1:T(8,128)}, u32[]{:S(2)}) copy-start(s32[64,6]{0,1:T(8,128)} %param.28) | copy-start | bytes 4612
  14.0 20.8 %all-to-all-start = ((bf16[64,2,240]{2,1,0:T(2,128)(2,1)}), bf16[64,2,240]{2,1,0:T(2,128)(2,1)S(1)}, u32[]{:S(2)}, u32[]{:S(2)}) async-start(bf16[64,2,240]{2,1,0:T(2,128)(2,1)} %reshape.3572), calls=%async_computation | async-start | bytes 131072 | tf_op jit(solution)/shard_map/all_to_all | solution.py:209
  27.3 15.9 %copy-start.20 = (pred[384]{0:T(512)(128)(4,1)}, pred[384]{0:T(512)(128)(4,1)S(1)}, u32[]{:S(2)}) copy-start(pred[384]{0:T(512)(128)(4,1)S(1)} %compare_and_fusion.1) | copy-start | bytes 1156
  27.4 13.7 %copy-start.17 = (s32[1024]{0:T(1024)}, s32[1024]{0:T(1024)S(1)}, u32[]{:S(2)}) copy-start(s32[1024]{0:T(1024)S(1)} %pad_clamp_fusion.1) | copy-start | bytes 12292
  50.1 13.4 %all-to-all-start.1 = ((bf16[64,2,240]{2,1,0:T(2,128)(2,1)}), bf16[64,2,240]{2,1,0:T(2,128)(2,1)S(1)}, u32[]{:S(2)}, u32[]{:S(2)}) async-start(bf16[64,2,240]{2,1,0:T(2,128)(2,1)} %reshape.3574), calls=%async_computation.1 | async-start | bytes 131072 | tf_op jit(solution)/shard_map/all_to_all | solution.py:216
  55.3 9.3 %copy-start.24 = (pred[6]{0:T(512)(128)(4,1)}, pred[6]{0:T(512)(128)(4,1)S(1)}, u32[]{:S(2)}) copy-start(pred[6]{0:T(512)(128)(4,1)S(1)} %dynamic-slice_reduce_fusion) | copy-start | bytes 22
  66.8 14.5 %copy-start.30 = (s32[64]{0:T(128)S(1)}, s32[64]{0:T(128)}, u32[]{:S(2)}) copy-start(s32[64]{0:T(128)} %param.26) | copy-start | bytes 772
  66.9 23.8 %copy-start.31 = (s32[64]{0:T(128)S(1)}, s32[64]{0:T(128)}, u32[]{:S(2)}) copy-start(s32[64]{0:T(128)} %param.29) | copy-start | bytes 772
  68.7 8.5 %all-to-all-start.2 = ((bf16[4,4,4,1,3,512]{5,2,4,3,1,0:T(4,128)(2,1)}), bf16[4,4,4,1,3,512]{5,2,4,3,1,0:T(4,128)(2,1)S(1)}, u32[]{:S(2)}, u32[]{:S(2)}) async-start(bf16[4,4,4,1,3,512]{5,2,4,3,1,0:T(4,128)(2,1)} %copy.197), calls=%async_computation.2 | async-start | bytes 393216 | tf_op jit(solution)/shard_map/all_to_all | solution.py:37
  77.9 8.5 %all-to-all-start.3 = ((bf16[4,4,4,1,3,512]{5,2,4,3,0,1:T(4,128)(2,1)}), bf16[4,4,4,1,3,512]{5,2,4,3,0,1:T(4,128)(2,1)S(1)}, u32[]{:S(2)}, u32[]{:S(2)}) async-start(bf16[4,4,4,1,3,512]{5,2,4,3,0,1:T(4,128)(2,1)} %copy.198), calls=%async_computation.3 | async-start | bytes 393216 | tf_op jit(solution)/shard_map/all_to_all | solution.py:37
  87.3 8.5 %all-to-all-start.4 = ((bf16[4,4,4,1,3,512]{5,1,4,3,0,2:T(4,128)(2,1)}), bf16[4,4,4,1,3,512]{5,1,4,3,0,2:T(4,128)(2,1)S(1)}, u32[]{:S(2)}, u32[]{:S(2)}) async-start(bf16[4,4,4,1,3,512]{5,1,4,3,0,2:T(4,128)(2,1)} %copy.199), calls=%async_computation.4 | async-start | bytes 393216 | tf_op jit(solution)/shard_map/all_to_all | solution.py:37
  95.9 25.3 %collective-permute-start = (bf16[64,3,512]{2,1,0:T(4,128)(2,1)S(1)}, bf16[64,3,512]{2,1,0:T(4,128)(2,1)S(1)}, u32[]{:S(2)}, u32[]{:S(2)}) collective-permute-start(bf16[64,3,512]{2,1,0:T(4,128)(2,1)S(1)} %bitcast.282), channel_id=1, source_target_pairs={{0,64},{64,0},{1,65},{65,1},{2,66},{66,2},{3,67},{67,3},{4,68},{68... | collective-permute-start | bytes 589832 | tf_op jit(solution)/shard_map/ppermute | solution.py:47
  120.1 15.8 %copy-start.22 = (pred[64]{0:T(512)(128)(4,1)}, pred[64]{0:T(512)(128)(4,1)S(1)}, u32[]{:S(2)}) copy-start(pred[64]{0:T(512)(128)(4,1)S(1)} %get-tuple-element.162) | copy-start | bytes 196
  120.1 15.8 %copy-start.19 = (s32[1024]{0:T(1024)}, s32[1024]{0:T(1024)S(1)}, u32[]{:S(2)}) copy-start(s32[1024]{0:T(1024)S(1)} %pad_clamp_fusion) | copy-start | bytes 12292
  144.7 2.6 copy-start.13
  151.7 2.1 copy-start
  153.7 1.1 copy-start.2
  153.8 1.3 copy-start.3
  153.8 1.3 copy-start.7
  153.8 1.3 copy-start.9
  153.8 1.3 copy-start.10
  179.9 2.7 copy-start.18
  181.9 2.9 %copy-start.21 = (pred[384]{0:T(512)(128)(4,1)S(1)}, pred[384]{0:T(512)(128)(4,1)}, u32[]{:S(2)}) copy-start(pred[384]{0:T(512)(128)(4,1)} %copy-done.20) | copy-start | bytes 1156
  204.6 0.7 copy-start.25
  206.5 31.0 %copy-start.23 = (pred[64]{0:T(512)(128)(4,1)S(1)}, pred[64]{0:T(512)(128)(4,1)}, u32[]{:S(2)}) copy-start(pred[64]{0:T(512)(128)(4,1)} %copy-done.22) | copy-start | bytes 196
  229.7 6.9 %collective-permute-start.1 = (bf16[64,3,512]{2,1,0:T(4,128)(2,1)S(1)}, bf16[64,3,512]{2,1,0:T(4,128)(2,1)S(1)}, u32[]{:S(2)}, u32[]{:S(2)}) collective-permute-start(bf16[64,3,512]{2,1,0:T(4,128)(2,1)S(1)} %bitcast.283), channel_id=1, source_target_pairs={{0,64},{64,0},{1,65},{65,1},{2,66},{66,2},{3,67},{67,3},{4,68},{68... | collective-permute-start | bytes 589832 | tf_op jit(solution)/shard_map/ppermute | solution.py:47
  260.2 2.6 copy-start.14
  267.1 2.1 copy-start.1
  269.2 1.1 copy-start.4
  269.3 1.3 copy-start.5
  269.3 1.3 copy-start.8
  269.3 1.3 copy-start.11
  269.3 1.3 copy-start.12
where the time goes:
time: 278 us; the launch traced here: 273 us
  local copies, waits for them, and re-layouts  89.1 us (32%)
  blocking collectives  76.4 us (27%)
  starting transfers between devices  57.2 us (21%)
  waiting for transfers between devices  31.7 us (11%)
  other arithmetic  15.4 us (6%)
    ppermute x2, starting transfers between devices, partner_2(): lax.ppermute(array, axis, [(i, i ^ 1 << stride) for i in range(lax.axis_s...  29.9 us
    all_to_all x2, blocking collectives, on_device(): lax.all_to_all(ordered, BLOCK, split_axis=0, concat_axis=2, tiled=True)  27.1 us
    all_to_all x3, blocking collectives, moved_by_axis(): result = lax.all_to_all(result, axes[k], k, k, tiled=True)  22.6 us
    unnamed x48, local copies, waits for them, and re-layouts  16 us
    convert_element_type x6, local copies, waits for them, and re-layouts, as_sent(): a.astype(jnp.bfloat16)  14.5 us
    all_to_all x3, waiting for transfers between devices, moved_by_axis(): result = lax.all_to_all(result, axes[k], k, k, tiled=True)  13.8 us
    all_to_all x1, blocking collectives, on_device(): lax.all_to_all(as_sent(face_cells), BLOCK, split_axis=3, concat_axis=0, t...  13.7 us
    all_to_all x1, blocking collectives, on_device(): lax.all_to_all(as_sent(chosen), BLOCK, split_axis=0, concat_axis=3, tiled...  13 us
  transfers between devices with their start and end apart: 7, of which 7 were waited for; matrix products, arithmetic and copies ran while one was open for 1% of the time, Pallas kernels for 0%

commit v1 on v0

v1 whole, which is shorter than its diff:
```python
import functools

import jax
import jax.numpy as jnp
from jax import lax
from jax.experimental import pallas as pl
from jax.experimental.pallas import tpu as pltpu
from jax.sharding import PartitionSpec as P

STEPS = 2
NB = 64
BS = 32
PAD = BS + 2
ROWS = PAD * 8
NCELL = 48
MESH = pl.DeviceIdType.MESH
F32 = jnp.float32
BF16 = jnp.bfloat16


def lookup(table, positions):
    hit = (positions[:, None] == lax.broadcasted_iota(jnp.int32, (1, NB), 1)).astype(jnp.int32)
    if table.ndim == 1:
        return jnp.sum(hit * table[None, :], axis=1)
    return jnp.sum(hit[:, :, None] * table[None], axis=1)


def invert(owner):
    slots = lax.broadcasted_iota(jnp.int32, (NB, NB), 0)
    blocks = lax.broadcasted_iota(jnp.int32, (NB, NB), 1)
    return jnp.sum(jnp.where(owner[None, :] == slots, blocks, 0), axis=1)


def make_tables(les_owner, ac_owner, les_nbr, ac_nbr, coupling):
    section = lax.axis_index("section")
    me = lax.axis_index("block")
    inv_les = invert(les_owner)
    inv_ac = invert(ac_owner)
    coupled = lookup(les_owner, lookup(coupling, inv_ac))
    feed = lookup(ac_owner, lookup(invert(coupling), inv_les))
    les_near = lookup(les_nbr, inv_les)
    ac_near = lookup(ac_nbr, inv_ac)
    cp_near = lookup(les_nbr, lookup(coupling, inv_ac))

    def slots_of(owner, near):
        return lookup(owner, near.reshape(-1)).reshape(NB, 6)

    axis_k = jnp.clip((me - NCELL) // 5, 0, 2)
    pick = lax.broadcasted_iota(jnp.int32, (1, 6), 1)

    def face(slots, d):
        return jnp.sum(jnp.where(pick == d, slots, 0), axis=1)

    own_slots = jnp.where(section == 0, slots_of(les_owner, les_near), slots_of(ac_owner, ac_near))
    cp_slots = slots_of(les_owner, cp_near)
    cells = jnp.where(section == 0, coupled, feed)
    is_cell = me < NCELL
    near = jnp.where(section == 0, les_near, ac_near)
    mine = lax.broadcasted_iota(jnp.int32, (NB, 1), 0) == me

    def flags(near):
        present = jnp.sum(jnp.where(mine, (near >= 0).astype(jnp.int32), 0), axis=0)
        return jnp.pad(present, (0, NB - 6))

    rows = [
        jnp.where(is_cell, cells, face(own_slots, 2 * axis_k)),
        jnp.where(is_cell, cells, face(own_slots, 2 * axis_k + 1)),
        face(cp_slots, 2 * axis_k),
        face(cp_slots, 2 * axis_k + 1),
        flags(near),
        flags(cp_near),
    ]
    return jnp.stack(rows, axis=0)


def kernel(tab, state_hbm, mean_hbm, out_hbm, q, acc, mean, ul, tile_a, recv_0, recv_1, sort_b, land, pick_ref,
           load_sem, loc_sem, sa, ra, sb, rb, rv, out_sem, side_sem):
    section = lax.axis_index("section")
    me = lax.axis_index("block")
    les = section == 0
    acoustic = section == 1
    q4 = q.reshape(5, PAD, 8, 128)
    acc4 = acc.reshape(5, BS, 8, 128)
    mean4 = mean.reshape(5, BS, 8, 128)

    def partner(n):
        return me ^ (n ^ 42)

    barrier = pltpu.get_barrier_semaphore()

    def greet(t, carry):
        pl.semaphore_signal(barrier, inc=1, device_id=(section, me ^ t), device_id_type=MESH)
        return carry

    pl.semaphore_signal(barrier, inc=1, device_id=(1 - section, me), device_id_type=MESH)
    lax.fori_loop(1, NB, greet, 0)

    recv_a = (recv_0, recv_1)

    def load_copy(c):
        return pltpu.make_async_copy(
            state_hbm.at[0, 0, :, :, pl.ds(128 * c, 128)], q4.at[:, pl.ds(1, BS), c, :], load_sem.at[0]
        )

    def mean_copy(c):
        return pltpu.make_async_copy(
            mean_hbm.at[0, :, :, pl.ds(128 * c, 128)], mean4.at[:, :, c, :], load_sem.at[1]
        )

    zero = jnp.zeros((8, 128), F32)
    for v in range(5):
        q[pl.ds(v * ROWS, 8), :] = zero
        q[pl.ds(v * ROWS + ROWS - 8, 8), :] = zero
    for c in range(8):
        load_copy(c).start()

    @pl.when(acoustic)
    def _():
        for c in range(8):
            mean_copy(c).start()

    lane = lax.broadcasted_iota(jnp.int32, (8, 128), 1)
    sub = lax.broadcasted_iota(jnp.int32, (8, 128), 0)
    zpos = lane % BS
    z_low = zpos == 0
    z_high = zpos == BS - 1
    even = lane % 2 == 0

    def up_y(v):
        r = pltpu.roll(v, 96, 1)
        return jnp.where(lane < 96, r, jnp.where(sub < 7, pltpu.roll(r, 7, 0), 0.0))

    def dn_y(v):
        r = pltpu.roll(v, 32, 1)
        return jnp.where(lane >= 32, r, jnp.where(sub > 0, pltpu.roll(r, 1, 0), 0.0))

    def up_z(v):
        return jnp.where(z_high, 0.0, pltpu.roll(v, 127, 1))

    def dn_z(v):
        return jnp.where(z_low, 0.0, pltpu.roll(v, 1, 1))

    lane_t = lax.broadcasted_iota(jnp.int32, (16, 128), 1)
    row_t = lax.broadcasted_iota(jnp.int32, (16, 128), 0)
    by_lane = jnp.where(lane_t % 2 == 1, 1.0, 0.0)
    by_row = jnp.where(row_t < 8, 1.0, 0.0)
    pick_ref[...] = jnp.where(me >= NCELL + 10, by_lane, by_row).astype(BF16)

    for s in range(STEPS):
        tile_a[s, NB - 1] = jnp.zeros((16, 128), BF16)
    loaded = q4.at[:, pl.ds(1, BS)]
    pltpu.make_async_copy(loaded, loaded, load_sem.at[0]).wait()

    def slab(v, x):
        return pl.ds(pl.multiple_of(v * ROWS + 8 * x + 8, 8), 8)

    def aslab(v, x):
        return pl.ds(pl.multiple_of(v * BS * 8 + 8 * x, 8), 8)

    @pl.when(les)
    def _():
        def prim(x, carry):
            inv = 1.0 / q[slab(0, x), :]
            for v in range(1, 4):
                q[slab(v, x), :] = q[slab(v, x), :] * inv
            return carry

        lax.fori_loop(0, BS, prim, 0, unroll=4)

    def pack(s):
        def cells(p, carry):
            for c in range(3):
                start = pl.multiple_of((c + 1) * ROWS + 16 * p + 8, 8)
                tile_a[s, c * 16 + p] = q[pl.ds(start, 16), :].astype(BF16)
            return carry

        lax.fori_loop(0, 16, cells, 0, unroll=4)

        def faces(v, carry):
            tile_a[s, NCELL + v] = jnp.concatenate(
                [q[slab(v, BS - 1), :], q[slab(v, 0), :]], axis=0
            ).astype(BF16)
            base = v * ROWS + 8
            low = high = zero
            for g in range(4):
                group = lane // 32 == g
                a = q[pl.ds(base + 64 * g, 8, stride=8), :]
                b = q[pl.ds(base + 64 * g + 7, 8, stride=8), :]
                low = jnp.where(group, a if g == 0 else pltpu.roll(a, 32 * g, 1), low)
                high = jnp.where(group, b if g == 3 else pltpu.roll(b, 32 * g + 32, 1), high)
            tile_a[s, NCELL + 5 + v] = jnp.concatenate([high, low], axis=0).astype(BF16)
            halves = []
            for half in range(2):
                packed = zero
                for x in range(16):
                    one = q[slab(v, 16 * half + x), :]
                    turned = one if x == 0 else pltpu.roll(one, 2 * x, 1)
                    packed = jnp.where(((lane + 1) % 32) // 2 == x, turned, packed)
                halves.append(packed)
            tile_a[s, NCELL + 10 + v] = jnp.concatenate(halves, axis=0).astype(BF16)
            return carry

        lax.fori_loop(0, 5, faces, 0)

    def send_a(s):
        def go(n, carry):
            j = partner(n)

            @pl.when(j != me)
            def _():
                pltpu.make_async_remote_copy(
                    src_ref=tile_a.at[s, j], dst_ref=recv_a[s].at[me], send_sem=sa.at[s], recv_sem=ra.at[s],
                    device_id=(section, j), device_id_type=MESH,
                ).start()

            @pl.when(j == me)
            def _():
                pltpu.make_async_copy(tile_a.at[s, me], recv_a[s].at[me], ra.at[s]).start()

            return carry

        lax.fori_loop(0, NB, go, 0)

    def les_terms(r, u, v, w, e, axis_k):
        vel = (u, v, w)
        m = (r * u, r * v, r * w)
        p = 0.4 * (e - 0.5 * (m[0] * u + m[1] * v + m[2] * w))
        speed = vel[axis_k]
        flux = [m[axis_k]] + [m[j] * speed + (p if j == axis_k else 0.0) for j in range(3)] + [(e + p) * speed]
        return (r,) + m + (e,), flux

    def les_interior():
        def body(x, carry):
            prev, plus = carry
            f = [q[slab(v, x), :] for v in range(5)]
            r, u, v_, w, e = f
            vel = (u, v_, w)
            m = (r * u, r * v_, r * w)
            p = 0.4 * (e - 0.5 * (m[0] * u + m[1] * v_ + m[2] * w))
            cons = (r,) + m + (e,)
            ep = e + p
            fluxes = []
            for k in range(3):
                sp = 0.1 * vel[k]
                fl = [0.1 * m[k]]
                for j in range(3):
                    t = m[j] * sp
                    if j == k:
                        t = t + 0.1 * p
                    fl.append(t)
                fl.append(ep * sp)
                fluxes.append(fl)
            new, nplus = [], []
            for i in range(5):
                d = 0.01 * cons[i]
                acc[aslab(i, jnp.maximum(x - 1, 0)), :] = prev[i] + (d - fluxes[0][i])
                total = 0.94 * cons[i] + plus[i]
                total = total + (up_y(d - fluxes[1][i]) + dn_y(d + fluxes[1][i]))
                total = total + (up_z(d - fluxes[2][i]) + dn_z(d + fluxes[2][i]))
                new.append(total)
                nplus.append(d + fluxes[0][i])
            return tuple(new), tuple(nplus)

        last, _ = lax.fori_loop(0, BS, body, ((zero,) * 5, (zero,) * 5))
        for i in range(5):
            acc[aslab(i, BS - 1), :] = last[i]

    def ac_interior():
        def body(x, carry):
            here = [q[slab(v, x), :] for v in range(5)]
            dx = [0.5 * (q[slab(v, x + 1), :] - q[slab(v, x - 1), :]) for v in range(5)]
            dy = [0.5 * (up_y(here[v]) - dn_y(here[v])) for v in range(5)]
            dz = [0.5 * (up_z(here[v]) - dn_z(here[v])) for v in range(5)]
            rho, wx, wy, wz, prs = [mean[aslab(v, x), :] for v in range(5)]
            inv = 1.0 / rho
            div = dx[1] + dy[2] + dz[3]
            adv = [wx * dx[v] + wy * dy[v] + wz * dz[v] for v in range(5)]
            extra = [rho * div, dx[4] * inv, dy[4] * inv, dz[4] * inv, (1.4 * prs) * div]
            for v in range(5):
                acc[aslab(v, x), :] = here[v] - 0.3 * (adv[v] + extra[v])
            return carry

        lax.fori_loop(0, BS, body, 0)

    def send_b(s):
        target = jnp.where(me < NCELL, 1 - section, section)
        face_id = me - NCELL
        axis_k = face_id // 5
        comp = face_id % 5 - 1
        tangential = les & (face_id >= 0) & (face_id < 15) & (comp >= 0) & (comp < 3) & (comp != axis_k)
        vel_slot = NB + jnp.maximum(2 * axis_k + comp - jnp.where(comp > axis_k, 1, 0), 0)
        from_low = pick_ref[...] > 0.5

        @pl.when(me != NB - 1)
        def _():
            def go(n, carry):
                dest = partner(n)
                sort_b[s, 0, dest] = jnp.where(from_low, recv_a[s][tab[0, dest]], recv_a[s][tab[1, dest]])
                local = (target == section) & (dest == me)

                @pl.when(jnp.logical_not(local))
                def _():
                    pltpu.make_async_remote_copy(
                        src_ref=sort_b.at[s, 0, dest], dst_ref=land.at[s, me], send_sem=sb.at[s],
                        recv_sem=rb.at[s], device_id=(target, dest), device_id_type=MESH,
                    ).start()

                @pl.when(local)
                def _():
                    pltpu.make_async_copy(sort_b.at[s, 0, dest], land.at[s, me], rb.at[s]).start()

                return carry

            lax.fori_loop(0, NB, go, 0)

        @pl.when(tangential)
        def _():
            def go(n, carry):
                dest = partner(n)
                sort_b[s, 1, dest] = jnp.where(from_low, recv_a[s][tab[2, dest]], recv_a[s][tab[3, dest]])
                pltpu.make_async_remote_copy(
                    src_ref=sort_b.at[s, 1, dest], dst_ref=land.at[s, vel_slot], send_sem=sb.at[STEPS + s],
                    recv_sem=rv.at[s], device_id=(1, dest), device_id_type=MESH,
                ).start()
                return carry

            lax.fori_loop(0, NB, go, 0)

        return tangential

    def tile(ref, *idx):
        return ref[idx].astype(F32)

    def halo_rows(s, axis_k, v):
        got = tile(land, s, NCELL + 5 * axis_k + v)
        own = tile(tile_a, s, NCELL + 5 * axis_k + v)
        low = jnp.where(tab[4, 2 * axis_k] > 0, got[:8], own[8:])
        high = jnp.where(tab[4, 2 * axis_k + 1] > 0, got[8:], own[:8])
        return low, high

    def turn_z(got, own, f_low, f_high):
        low = jnp.where(f_low > 0, pltpu.roll(got, 97, 1), own)
        high = jnp.where(f_high > 0, pltpu.roll(got, 31, 1), own)
        return jnp.where(even, low, high)

    def halo_z(s, v):
        got = tile(land, s, NCELL + 10 + v)
        own = tile(tile_a, s, NCELL + 10 + v)
        return [turn_z(got[8 * h:8 * h + 8], own[8 * h:8 * h + 8], tab[4, 4], tab[4, 5]) for h in range(2)]

    def les_finish(s, last):
        def side_terms(h, axis_k, sign):
            cons, flux = les_terms(*h, axis_k)
            return [0.01 * c + sign * f for c, f in zip(cons, flux)]

        pairs = [halo_rows(s, 0, v) for v in range(5)]
        for side, x, sign in ((0, 0, 0.1), (1, BS - 1, -0.1)):
            terms = side_terms([pr[side] for pr in pairs], 0, sign)
            for v in range(5):
                acc[aslab(v, x), :] = acc[aslab(v, x), :] + terms[v]
        pairs = [halo_rows(s, 1, v) for v in range(5)]
        for side, row, sign in ((0, 0, 0.1), (1, 7, -0.1)):
            terms = side_terms([pr[side] for pr in pairs], 1, sign)
            keep = lane < 32 if side == 0 else lane >= 96
            for v in range(5):
                for g in range(4):
                    amount = (128 - 32 * g if side == 0 else 96 - 32 * g) % 128
                    t = terms[v] if amount == 0 else pltpu.roll(terms[v], amount, 1)
                    where = pl.ds(v * BS * 8 + 64 * g + row, 8, stride=8)
                    acc[where, :] = acc[where, :] + jnp.where(keep, t, 0.0)
        zs = [halo_z(s, v) for v in range(5)]
        sign = jnp.where(even, 0.1, -0.1)
        edge = z_low | z_high
        for half in range(2):
            terms = side_terms([z[half] for z in zs], 2, sign)
            for p in range(8):
                back = [tile(land, s, c * 16 + 8 * half + p) for c in range(3)]
                for o in range(2):
                    x = 16 * half + 2 * p + o
                    new = []
                    for v in range(5):
                        amount = (128 - 2 * (2 * p + o)) % 128
                        t = terms[v] if amount == 0 else pltpu.roll(terms[v], amount, 1)
                        val = acc[aslab(v, x), :] + jnp.where(edge, t, 0.0)
                        if 1 <= v <= 3:
                            val = val + 0.1 * back[v - 1][8 * o:8 * o + 8]
                        new.append(val)
                    if not last:
                        inv = 1.0 / new[0]
                        new = [new[0]] + [new[v] * inv for v in range(1, 4)] + [new[4]]
                    for v in range(5):
                        q[slab(v, x), :] = new[v]

    def ac_finish(s):
        half_dt = 0.15
        UROWS = PAD * 8

        def uslab(c, x):
            return pl.ds(pl.multiple_of(c * UROWS + 8 * x + 8, 8), 8)

        def unpack(p, carry):
            for c in range(3):
                ul[pl.ds(pl.multiple_of(c * UROWS + 16 * p + 8, 8), 16), :] = tile(land, s, c * 16 + p)
            return carry

        lax.fori_loop(0, 16, unpack, 0, unroll=4)

        pairs = [halo_rows(s, 0, v) for v in range(5)]

        def side_terms(h, m, axis_k, alpha):
            rho, wx, wy, wz, prs = m
            w = (wx, wy, wz)[axis_k]
            terms = [w * h[v] for v in range(5)]
            terms[0] = terms[0] + rho * h[1 + axis_k]
            terms[1 + axis_k] = terms[1 + axis_k] + h[4] / rho
            terms[4] = terms[4] + (1.4 * prs) * h[1 + axis_k]
            return [alpha * t for t in terms]

        for side, x, alpha in ((0, 0, half_dt), (1, BS - 1, -half_dt)):
            m = [mean[aslab(v, x), :] for v in range(5)]
            terms = side_terms([pr[side] for pr in pairs], m, 0, alpha)
            for v in range(5):
                acc[aslab(v, x), :] = acc[aslab(v, x), :] + terms[v]
        pairs_y = [halo_rows(s, 1, v) for v in range(5)]
        zs = [halo_z(s, v) for v in range(5)]

        vel_count = land.at[s, pl.ds(NB, 6)]
        pltpu.make_async_copy(vel_count, vel_count, rv.at[s]).wait()

        vx = [tile(land, s, NB + o) for o in range(2)]
        for o, c in enumerate((1, 2)):
            ul[uslab(c, -1), :] = jnp.where(tab[5, 0] > 0, vx[o][:8], ul[uslab(c, 0), :])
            ul[uslab(c, BS), :] = jnp.where(tab[5, 1] > 0, vx[o][8:], ul[uslab(c, BS - 1), :])

        vy = [tile(land, s, NB + 2 + o) for o in range(2)]
        for side, row, alpha in ((0, 0, half_dt), (1, 7, -half_dt)):
            keep = lane < 32 if side == 0 else lane >= 96
            for g in range(4):
                amount = (128 - 32 * g if side == 0 else 96 - 32 * g) % 128

                def turned(t):
                    return t if amount == 0 else pltpu.roll(t, amount, 1)

                def strided(rows, v, lead):
                    return pl.ds(v * rows + lead + 64 * g + row, 8, stride=8)

                m = [mean[strided(BS * 8, v, 0), :] for v in range(5)]
                h = [turned(pr[side]) for pr in pairs_y]
                terms = side_terms(h, m, 1, alpha)
                u = [ul[strided(UROWS, c, 8), :] for c in range(3)]
                hx, hz = [
                    jnp.where(tab[5, 2 + side] > 0, turned(vy[o][8 * side:8 * side + 8]), u[c])
                    for o, c in enumerate((0, 2))
                ]
                terms[1] = terms[1] + alpha * (u[1] * hx)
                terms[2] = terms[2] - alpha * (hx * u[0] + hz * u[2])
                terms[3] = terms[3] + alpha * (u[1] * hz)
                for v in range(5):
                    where = strided(BS * 8, v, 0)
                    acc[where, :] = acc[where, :] + jnp.where(keep, terms[v], 0.0)

        vz = [tile(land, s, NB + 4 + o) for o in range(2)]
        edge = z_low | z_high
        alpha_z = jnp.where(z_low, half_dt, -half_dt)
        for half in range(2):
            for xx in range(16):
                x = 16 * half + xx
                amount = (128 - 2 * xx) % 128

                def turned(t):
                    return t if amount == 0 else pltpu.roll(t, amount, 1)

                m = [mean[aslab(v, x), :] for v in range(5)]
                h = [turned(zs[v][half]) for v in range(5)]
                terms = side_terms(h, m, 2, alpha_z)
                u = [ul[uslab(c, x), :] for c in range(3)]
                dxv, dxw = [0.5 * (ul[uslab(c, x + 1), :] - ul[uslab(c, x - 1), :]) for c in (1, 2)]
                dyu, dyw = [0.5 * (up_y(u[c]) - dn_y(u[c])) for c in (0, 2)]
                dz = []
                for o, c in enumerate((0, 1)):
                    got = vz[o][8 * half:8 * half + 8]
                    low = pltpu.roll(got, (97 + amount) % 128, 1)
                    high = pltpu.roll(got, (31 + amount) % 128, 1)
                    low = jnp.where(tab[5, 4] > 0, low, u[c])
                    high = jnp.where(tab[5, 5] > 0, high, u[c])
                    dz.append(0.5 * (jnp.where(z_high, high, pltpu.roll(u[c], 127, 1))
                                     - jnp.where(z_low, low, pltpu.roll(u[c], 1, 1))))
                dzu, dzv = dz
                ox, oy, oz = dyw - dzv, dzu - dxw, dxv - dyu
                lamb = (oy * u[2] - oz * u[1], oz * u[0] - ox * u[2], ox * u[1] - oy * u[0])
                for v in range(5):
                    val = acc[aslab(v, x), :] + jnp.where(edge, terms[v], 0.0)
                    if 1 <= v <= 3:
                        val = val - 0.3 * lamb[v - 1]
                    q[slab(v, x), :] = val

    pack(0)
    pl.semaphore_wait(barrier, NB)
    pl.semaphore_signal(side_sem, inc=1, device_id=(1 - section, me), device_id_type=MESH)
    send_a(0)

    @pl.when(acoustic)
    def _():
        pltpu.make_async_copy(mean4, mean4, load_sem.at[1]).wait()

    for s in range(STEPS):
        if s:
            pack(s)
            send_a(s)

        @pl.when(les)
        def _():
            les_interior()

        @pl.when(acoustic)
        def _():
            ac_interior()

        if s == 0:
            pl.semaphore_wait(side_sem, 1)
        pltpu.make_async_copy(recv_a[s], recv_a[s], ra.at[s]).wait()
        tangential = send_b(s)
        got = land.at[s, pl.ds(0, NB - 1)]
        pltpu.make_async_copy(got, got, rb.at[s]).wait()

        @pl.when(les)
        def _():
            les_finish(s, s == STEPS - 1)

        @pl.when(acoustic)
        def _():
            ac_finish(s)

    def out_copy(c):
        return pltpu.make_async_copy(
            q4.at[:, pl.ds(1, BS), c, :], out_hbm.at[0, 0, :, :, pl.ds(128 * c, 128)], out_sem
        )

    for c in range(8):
        out_copy(c).start()
    for s in range(STEPS):
        sent = tile_a.at[s, pl.ds(0, NB - 1)]
        pltpu.make_async_copy(sent, sent, sa.at[s]).wait()

        @pl.when(me != NB - 1)
        def _():
            everyone = sort_b.at[s, 0]
            others = sort_b.at[s, 0, pl.ds(0, NB - 1)]

            @pl.when(me < NCELL)
            def _():
                pltpu.make_async_copy(everyone, everyone, sb.at[s]).wait()

            @pl.when(me >= NCELL)
            def _():
                pltpu.make_async_copy(others, others, sb.at[s]).wait()

        @pl.when(tangential)
        def _():
            extra = sort_b.at[s, 1]
            pltpu.make_async_copy(extra, extra, sb.at[STEPS + s]).wait()

    final = q4.at[:, pl.ds(1, BS)]
    pltpu.make_async_copy(final, final, out_sem).wait()


def on_device(state, mean_flow, les_owner, ac_owner, les_nbr, ac_nbr, coupling):
    tables = make_tables(les_owner, ac_owner, les_nbr, ac_nbr, coupling)
    hbm = pl.BlockSpec(memory_space=pl.ANY)
    return pl.pallas_call(
        kernel,
        out_shape=jax.ShapeDtypeStruct(state.shape, F32),
        in_specs=[pl.BlockSpec(memory_space=pltpu.SMEM), hbm, hbm],
        out_specs=hbm,
        scratch_shapes=[
            pltpu.VMEM((5 * ROWS, 128), F32),
            pltpu.VMEM((5 * BS * 8, 128), F32),
            pltpu.VMEM((5 * BS * 8, 128), F32),
            pltpu.VMEM((3 * ROWS, 128), F32),
            pltpu.VMEM((STEPS, NB, 16, 128), BF16),
            pltpu.VMEM((NB, 16, 128), BF16),
            pltpu.VMEM((NB, 16, 128), BF16),
            pltpu.VMEM((STEPS, 2, NB, 16, 128), BF16),
            pltpu.VMEM((STEPS, NB + 6, 16, 128), BF16),
            pltpu.VMEM((16, 128), BF16),
            pltpu.SemaphoreType.DMA((2,)),
            pltpu.SemaphoreType.DMA((1,)),
            pltpu.SemaphoreType.DMA((STEPS,)),
            pltpu.SemaphoreType.DMA((STEPS,)),
            pltpu.SemaphoreType.DMA((2 * STEPS,)),
            pltpu.SemaphoreType.DMA((STEPS,)),
            pltpu.SemaphoreType.DMA((STEPS,)),
            pltpu.SemaphoreType.DMA(()),
            pltpu.SemaphoreType.REGULAR,
        ],
        compiler_params=pltpu.CompilerParams(
            collective_id=0, has_side_effects=True, vmem_limit_bytes=24 << 20
        ),
    )(tables, state, mean_flow)


def solution(mesh):
    placed = (P("section", "block"), P("block"), P(), P(), P(), P(), P())
    return jax.shard_map(
        on_device, mesh=mesh, in_specs=placed, out_specs=P("section", "block"), check_vma=False
    )
```

time: 278 us -> 51.9 us (0.19); the launches traced: 273 us -> 51.7 us
  local copies, waits for them, and re-layouts: 89.1 us -> 3.08 us
  blocking collectives: 76.4 us -> 0 us
  starting transfers between devices: 57.2 us -> 0 us
  Pallas kernels: 0 us -> 41.1 us
  waiting for transfers between devices: 31.7 us -> 0 us
  other arithmetic: 15.4 us -> 7.4 us
    all_to_all x7 -> x0, blocking collectives: 76.4 us -> none  [the longest x2 27.1 us: on_device(): lax.all_to_all(ordered, BLOCK, split_axis=0, concat_axis=2, tiled=True)]
    pallas_call x0 -> x1, Pallas kernels: none -> 41.1 us  [on_device(): pl.pallas_call(kernel, out_shape=jax.ShapeDtypeStruct(state.shape, F32),...]
    ppermute x2 -> x0, starting transfers between devices: 29.9 us -> none  [partner_2(): lax.ppermute(array, axis, [(i, i ^ 1 << stride) for i in range(lax.axis_s...]
    all_to_all x5 -> x0, waiting for transfers between devices: 29.5 us -> none  [the longest x3 13.8 us: moved_by_axis(): result = lax.all_to_all(result, axes[k], k, k, tiled=True)]
    all_to_all x5 -> x0, starting transfers between devices: 27.3 us -> none  [the longest x1 12.3 us: on_device(): lax.all_to_all(as_sent(face_cells), BLOCK, split_axis=3, concat_axis=0, t...]
    slice x19 -> x0, local copies, waits for them, and re-layouts: 18.6 us -> none  [the longest x2 4.31 us: face_grid(): halo_cells[:, direction].reshape(num_blocks, num_vars, cube_side, cube_side)]
    convert_element_type x14 -> x0, local copies, waits for them, and re-layouts: 17.1 us -> none  [the longest x6 14.5 us: as_sent(): a.astype(jnp.bfloat16)]
    broadcast_in_dim x8 -> x0, local copies, waits for them, and re-layouts: 14.6 us -> none  [the longest x4 7.3 us: neighbours(): jnp.repeat(face_grid(4), cube_side, axis=3)]
  transfers between devices with their start and end apart: 7 -> 0, of which waited for: 7 -> 0; matrix products, arithmetic and copies ran while one was open for 1% -> 0% of each run, Pallas kernels for 0% -> 0%
where the time goes in v1:
time: 51.9 us; the launch traced here: 51.7 us
  Pallas kernels  41.1 us (79%)
  other arithmetic  7.4 us (14%)
  local copies, waits for them, and re-layouts  3.08 us (6%)
    pallas_call x1, Pallas kernels, on_device(): pl.pallas_call(kernel, out_shape=jax.ShapeDtypeStruct(state.shape, F32),...  41.1 us
    reduce_sum x6, other arithmetic, lookup(): return jnp.sum(hit * table[None, :], axis=1)  4.22 us
    unnamed x5, local copies, waits for them, and re-layouts  1.93 us
    reduce_sum x2, other arithmetic, lookup(): return jnp.sum(hit[:, :, None] * table[None], axis=1)  1.84 us

profile of v1, /device:TPU:1, one launch (start us, length us, event | category | flops | bytes accessed | tf_op | source)
XLA Modules:
  0.0 51.7 jit_solution(8583855419894531179)
XLA Ops:
  0.0 0.0 copy-start
  0.0 0.8 %select_reduce_fusion.5 = (s32[64]{0:T(128)S(1)}, s32[64]{0:T(128)S(1)}) fusion(s32[64]{0:T(128)} %param.13, s32[64]{0:T(128)} %param.9), kind=kLoop, calls=%fused_computation.12 | loop fusion | flops 24448 | bytes 1024 | tf_op jit(solution)/shard_map/reduce_sum | solution.py:31
  0.9 0.2 select_reduce_fusion.4
  1.1 0.8 %select_reduce_fusion.3 = (s32[64]{0:T(128)S(1)}, s32[64]{0:T(128)S(1)}) fusion(s32[64]{0:T(128)S(1)} %select_reduce_fusion.4, s32[64]{0:T(128)} %param.10), kind=kLoop, calls=%fused_computation.9 | loop fusion | flops 24448 | bytes 1024 | tf_op jit(solution)/shard_map/reduce_sum | solution.py:24
  1.9 0.8 %select_reduce_fusion.8 = s32[64]{0:T(128)S(1)} fusion(s32[64]{0:T(128)} %param.13, s32[64]{0:T(128)S(1)} %get-tuple-element.18), kind=kLoop, calls=%fused_computation.21 | loop fusion | flops 12224 | bytes 768 | tf_op jit(solution)/shard_map/reduce_sum | solution.py:24
  2.8 0.8 %select_reduce_fusion.7 = s32[64]{0:T(128)S(1)} fusion(s32[64]{0:T(128)} %param.9, s32[64]{0:T(128)S(1)} %select_reduce_fusion.8), kind=kLoop, calls=%fused_computation.18 | loop fusion | flops 12224 | bytes 768 | tf_op jit(solution)/shard_map/reduce_sum | solution.py:24
  3.6 0.1 fusion.1
  3.7 0.1 fusion.2
  3.8 0.9 %multiply_reduce_fusion.1 = s32[64,6]{0,1:T(8,128)S(1)} fusion(s32[64,6]{0,1:T(8,128)} %param.12, s32[64,64]{1,0:T(8,128)S(1)} %fusion.2), kind=kLoop, calls=%fused_computation.1 | loop fusion | flops 48768 | bytes 19456 | tf_op jit(solution)/shard_map/reduce_sum | solution.py:25
  4.6 0.1 fusion
  4.7 1.0 %multiply_reduce_fusion = (s32[64,6]{0,1:T(8,128)S(1)}, s32[64,6]{0,1:T(8,128)S(1)}) fusion(s32[64,64]{1,0:T(8,128)S(1)} %fusion.1, s32[64,6]{0,1:T(8,128)} %param.11, s32[64,64]{1,0:T(8,128)S(1)} %fusion), kind=kLoop, calls=%fused_computation | loop fusion | flops 97536 | bytes 37376 | tf_op jit(solution)/shard_map/reduce_sum | solution.py:25
  5.7 0.2 select_reduce_fusion.10
  5.8 0.1 copy.13
  5.9 0.1 eq.222
  6.1 0.8 %select_reduce_fusion.1 = s32[384]{0:T(512)S(1)} fusion(s32[64]{0:T(128)} %param.10, s32[384]{0:T(512)S(1)} %eq.222), kind=kLoop, calls=%fused_computation.5 | loop fusion | flops 73344 | bytes 3328 | tf_op jit(solution)/shard_map/reduce_sum | solution.py:24
  6.8 0.1 copy.12
  6.9 0.1 eq.218
  7.1 0.1 copy.16
  7.2 0.1 eq.228
  7.3 0.8 %select_reduce_fusion = (s32[384]{0:T(512)S(1)}, s32[384]{0:T(512)S(1)}) fusion(s32[384]{0:T(512)S(1)} %eq.228, s32[64]{0:T(128)} %param.9, s32[384]{0:T(512)S(1)} %eq.218), kind=kLoop, calls=%fused_computation.3 | loop fusion | flops 146688 | bytes 6400 | tf_op jit(solution)/shard_map/reduce_sum | solution.py:24
  8.1 0.1 select_n.111
  8.2 0.1 copy.14
  8.3 0.1 reshape.134
  8.4 0.1 copy.17
  8.5 0.1 select_reduce_fusion.14
  8.7 0.0 copy-done
  8.7 0.0 copy-start.1
  8.7 1.1 %copy-done.1 = f32[1,5,32,1024]{3,2,1,0:T(8,128)S(1)} copy-done((f32[1,5,32,1024]{3,2,1,0:T(8,128)S(1)}, f32[1,5,32,1024]{3,2,1,0:T(8,128)}, u32[]{:S(2)}) %copy-start.1) | copy-done | bytes 655384
  9.8 41.1 %shard_map.73 = f32[1,1,5,32,1024]{4,3,2,1,0:T(8,128)S(1)} custom-call(s32[6,64]{1,0:T(8,128)S(1)} %stack.21.tab, f32[1,1,5,32,1024]{4,3,2,1,0:T(8,128)S(1)} %copy-done, f32[1,5,32,1024]{3,2,1,0:T(8,128)S(1)} %copy-done.1), custom_call_target="tpu_custom_call" | custom-call | tf_op jit(solution)/shard_map/pallas_call | solution.py:570
  50.8 0.8 %copy.20 = f32[1,1,5,32,1024]{4,3,2,1,0:T(8,128)} copy(f32[1,1,5,32,1024]{4,3,2,1,0:T(8,128)S(1)} %shard_map.73) | data formatting | bytes 1310720
  (7 shorter events, 0.1 us)
Async XLA Ops:
  0.0 8.7 %copy-start = (f32[1,1,5,32,1024]{4,3,2,1,0:T(8,128)S(1)}, f32[1,1,5,32,1024]{4,3,2,1,0:T(8,128)}, u32[]{:S(2)}) copy-start(f32[1,1,5,32,1024]{4,3,2,1,0:T(8,128)} %state_hbm.1) | copy-start | bytes 1966084
  8.7 1.1 %copy-start.1 = (f32[1,5,32,1024]{3,2,1,0:T(8,128)S(1)}, f32[1,5,32,1024]{3,2,1,0:T(8,128)}, u32[]{:S(2)}) copy-start(f32[1,5,32,1024]{3,2,1,0:T(8,128)} %mean_hbm.1) | copy-start | bytes 1966084

commit v2 on v1

--- a/solution.py
+++ b/solution.py
@@ -18,63 +18,8 @@
 BF16 = jnp.bfloat16
 
 
-def lookup(table, positions):
-    hit = (positions[:, None] == lax.broadcasted_iota(jnp.int32, (1, NB), 1)).astype(jnp.int32)
-    if table.ndim == 1:
-        return jnp.sum(hit * table[None, :], axis=1)
-    return jnp.sum(hit[:, :, None] * table[None], axis=1)
-
-
-def invert(owner):
-    slots = lax.broadcasted_iota(jnp.int32, (NB, NB), 0)
-    blocks = lax.broadcasted_iota(jnp.int32, (NB, NB), 1)
-    return jnp.sum(jnp.where(owner[None, :] == slots, blocks, 0), axis=1)
-
-
-def make_tables(les_owner, ac_owner, les_nbr, ac_nbr, coupling):
-    section = lax.axis_index("section")
-    me = lax.axis_index("block")
-    inv_les = invert(les_owner)
-    inv_ac = invert(ac_owner)
-    coupled = lookup(les_owner, lookup(coupling, inv_ac))
-    feed = lookup(ac_owner, lookup(invert(coupling), inv_les))
-    les_near = lookup(les_nbr, inv_les)
-    ac_near = lookup(ac_nbr, inv_ac)
-    cp_near = lookup(les_nbr, lookup(coupling, inv_ac))
-
-    def slots_of(owner, near):
-        return lookup(owner, near.reshape(-1)).reshape(NB, 6)
-
-    axis_k = jnp.clip((me - NCELL) // 5, 0, 2)
-    pick = lax.broadcasted_iota(jnp.int32, (1, 6), 1)
-
-    def face(slots, d):
-        return jnp.sum(jnp.where(pick == d, slots, 0), axis=1)
-
-    own_slots = jnp.where(section == 0, slots_of(les_owner, les_near), slots_of(ac_owner, ac_near))
-    cp_slots = slots_of(les_owner, cp_near)
-    cells = jnp.where(section == 0, coupled, feed)
-    is_cell = me < NCELL
-    near = jnp.where(section == 0, les_near, ac_near)
-    mine = lax.broadcasted_iota(jnp.int32, (NB, 1), 0) == me
-
-    def flags(near):
-        present = jnp.sum(jnp.where(mine, (near >= 0).astype(jnp.int32), 0), axis=0)
-        return jnp.pad(present, (0, NB - 6))
-
-    rows = [
-        jnp.where(is_cell, cells, face(own_slots, 2 * axis_k)),
-        jnp.where(is_cell, cells, face(own_slots, 2 * axis_k + 1)),
-        face(cp_slots, 2 * axis_k),
-        face(cp_slots, 2 * axis_k + 1),
-        flags(near),
-        flags(cp_near),
-    ]
-    return jnp.stack(rows, axis=0)
-
-
-def kernel(tab, state_hbm, mean_hbm, out_hbm, q, acc, mean, ul, tile_a, recv_0, recv_1, sort_b, land, pick_ref,
-           load_sem, loc_sem, sa, ra, sb, rb, rv, out_sem, side_sem):
+def kernel(les_owner, ac_owner, coupling, les_nbr, ac_nbr, state_hbm, mean_hbm, out_ref, q, acc, mean, ul, tile_a, recv_0, recv_1, sort_b, land, pick_ref,
+           list_0, list_1, list_2, near_0, near_1, idx_v, tab_v, tab, idx_sem, load_sem, tab_sem, sa, ra, sb, rb, rv, side_sem):
     section = lax.axis_index("section")
     me = lax.axis_index("block")
     les = section == 0
@@ -88,12 +33,15 @@
 
     barrier = pltpu.get_barrier_semaphore()
 
-    def greet(t, carry):
-        pl.semaphore_signal(barrier, inc=1, device_id=(section, me ^ t), device_id_type=MESH)
+    def greet(n, carry):
+        @pl.when(n != 42)
+        def _():
+            pl.semaphore_signal(barrier, inc=1, device_id=(section, partner(n)), device_id_type=MESH)
+
         return carry
 
+    lax.fori_loop(0, NB, greet, 0)
     pl.semaphore_signal(barrier, inc=1, device_id=(1 - section, me), device_id_type=MESH)
-    lax.fori_loop(1, NB, greet, 0)
 
     recv_a = (recv_0, recv_1)
 
@@ -113,6 +61,13 @@
         q[pl.ds(v * ROWS + ROWS - 8, 8), :] = zero
     for c in range(8):
         load_copy(c).start()
+    lists = (list_0, list_1, list_2, near_0, near_1)
+    idx_copies = [
+        pltpu.make_async_copy(ref, lists[i], idx_sem.at[i])
+        for i, ref in enumerate((les_owner, ac_owner, coupling, les_nbr, ac_nbr))
+    ]
+    for copy in idx_copies:
+        copy.start()
 
     @pl.when(acoustic)
     def _():
@@ -144,6 +99,7 @@
     row_t = lax.broadcasted_iota(jnp.int32, (16, 128), 0)
     by_lane = jnp.where(lane_t % 2 == 1, 1.0, 0.0)
     by_row = jnp.where(row_t < 8, 1.0, 0.0)
+    idx_v[...] = jnp.zeros((24, 128), jnp.int32)
     pick_ref[...] = jnp.where(me >= NCELL + 10, by_lane, by_row).astype(BF16)
 
     for s in range(STEPS):
@@ -166,6 +122,65 @@
             return carry
 
         lax.fori_loop(0, BS, prim, 0, unroll=4)
+
+    def make_tables():
+        row = lax.broadcasted_iota(jnp.int32, (NB, 128), 0)
+        col = lax.broadcasted_iota(jnp.int32, (NB, 128), 1)
+
+        def over_lanes(a):
+            for shift in (1, 2, 4, 8, 16, 32, 64):
+                a = a + pltpu.roll(a, shift, 1)
+            return a
+
+        def over_rows(a):
+            total = a[:8]
+            for i in range(1, 8):
+                total = total + a[8 * i:8 * i + 8]
+            for shift in (1, 2, 4):
+                total = total + pltpu.roll(total, shift, 0)
+            return total
+
+        def wide(a):
+            return jnp.concatenate([a] * 8, axis=0)
+
+        def column(i):
+            line = jnp.broadcast_to(idx_v[pl.ds(i, 1), :], (NB, 128))
+            return over_lanes(jnp.where(row == col, line, 0))
+
+        def look(column_table, index_row):
+            return over_rows(jnp.where(row == wide(index_row), column_table, 0))
+
+        les_col, ac_col, link_col = column(0), column(1), column(2)
+        own_col = jnp.where(les, les_col, ac_col)
+        near_at = jnp.where(les, 8, 16)
+        inv_own = over_rows(jnp.where(own_col == col, row, 0))
+        inv_ac = over_rows(jnp.where(ac_col == col, row, 0))
+        linked = look(link_col, inv_ac)
+        coupled = look(les_col, linked)
+        inv_les = over_rows(jnp.where(les_col == col, row, 0))
+        feed = over_rows(jnp.where(link_col == wide(inv_les), ac_col, 0))
+        cells = jnp.where(les, coupled, feed)
+        axis_k = jnp.maximum(me - NCELL, 0) // 5
+        rows = []
+        for side in range(2):
+            d = 2 * axis_k + side
+            near_col = column(near_at + d)
+            first = jnp.where(me < NCELL, cells, look(own_col, look(near_col, inv_own)))
+            second = look(own_col, look(near_col, linked))
+            rows.append((first, second))
+        own_row = idx_v[pl.ds(jnp.where(les, 0, 1), 1), :]
+        linked_me = over_rows(jnp.where(ac_col == me, link_col, 0))
+        own_near = idx_v[pl.ds(pl.multiple_of(near_at, 8), 8), :]
+        in_use = lane < NB
+        mine = over_lanes(jnp.where((own_row == me) & in_use, own_near, 0))
+        theirs = over_lanes(jnp.where((lane == linked_me) & in_use, idx_v[8:16, :], 0))
+        out = jnp.zeros((8, 128), jnp.int32)
+        for i, part in enumerate([rows[0][0], rows[1][0], rows[0][1], rows[1][1]]):
+            out = jnp.where(sub == i, part, out)
+        tab_v[0:8, :] = out
+        tab_v[8:16, :] = mine
+        tab_v[16:24, :] = theirs
+        pltpu.make_async_copy(tab_v, tab, tab_sem).start()
 
     def pack(s):
         def cells(p, carry):
@@ -220,6 +235,12 @@
             return carry
 
         lax.fori_loop(0, NB, go, 0)
+
+    def put(v, x, value, last):
+        if last:
+            out_ref[pl.ds(v * BS * 8 + 64 * (x // 8) + x % 8, 8, stride=8), :] = value
+        else:
+            q[slab(v, x), :] = value
 
     def les_terms(r, u, v, w, e, axis_k):
         vel = (u, v, w)
@@ -309,19 +330,14 @@
                 def _():
                     pltpu.make_async_copy(sort_b.at[s, 0, dest], land.at[s, me], rb.at[s]).start()
 
-                return carry
-
-            lax.fori_loop(0, NB, go, 0)
-
-        @pl.when(tangential)
-        def _():
-            def go(n, carry):
-                dest = partner(n)
-                sort_b[s, 1, dest] = jnp.where(from_low, recv_a[s][tab[2, dest]], recv_a[s][tab[3, dest]])
-                pltpu.make_async_remote_copy(
-                    src_ref=sort_b.at[s, 1, dest], dst_ref=land.at[s, vel_slot], send_sem=sb.at[STEPS + s],
-                    recv_sem=rv.at[s], device_id=(1, dest), device_id_type=MESH,
-                ).start()
+                @pl.when(tangential)
+                def _():
+                    sort_b[s, 1, dest] = jnp.where(from_low, recv_a[s][tab[2, dest]], recv_a[s][tab[3, dest]])
+                    pltpu.make_async_remote_copy(
+                        src_ref=sort_b.at[s, 1, dest], dst_ref=land.at[s, vel_slot], send_sem=sb.at[STEPS + s],
+                        recv_sem=rv.at[s], device_id=(1, dest), device_id_type=MESH,
+                    ).start()
+
                 return carry
 
             lax.fori_loop(0, NB, go, 0)
@@ -334,19 +350,19 @@
     def halo_rows(s, axis_k, v):
         got = tile(land, s, NCELL + 5 * axis_k + v)
         own = tile(tile_a, s, NCELL + 5 * axis_k + v)
-        low = jnp.where(tab[4, 2 * axis_k] > 0, got[:8], own[8:])
-        high = jnp.where(tab[4, 2 * axis_k + 1] > 0, got[8:], own[:8])
+        low = jnp.where(tab[8 + 2 * axis_k, 0] >= 0, got[:8], own[8:])
+        high = jnp.where(tab[9 + 2 * axis_k, 0] >= 0, got[8:], own[:8])
         return low, high
 
     def turn_z(got, own, f_low, f_high):
-        low = jnp.where(f_low > 0, pltpu.roll(got, 97, 1), own)
-        high = jnp.where(f_high > 0, pltpu.roll(got, 31, 1), own)
+        low = jnp.where(f_low >= 0, pltpu.roll(got, 97, 1), own)
+        high = jnp.where(f_high >= 0, pltpu.roll(got, 31, 1), own)
         return jnp.where(even, low, high)
 
     def halo_z(s, v):
         got = tile(land, s, NCELL + 10 + v)
         own = tile(tile_a, s, NCELL + 10 + v)
-        return [turn_z(got[8 * h:8 * h + 8], own[8 * h:8 * h + 8], tab[4, 4], tab[4, 5]) for h in range(2)]
+        return [turn_z(got[8 * h:8 * h + 8], own[8 * h:8 * h + 8], tab[12, 0], tab[13, 0]) for h in range(2)]
 
     def les_finish(s, last):
         def side_terms(h, axis_k, sign):
@@ -389,9 +405,9 @@
                         inv = 1.0 / new[0]
                         new = [new[0]] + [new[v] * inv for v in range(1, 4)] + [new[4]]
                     for v in range(5):
-                        q[slab(v, x), :] = new[v]
-
-    def ac_finish(s):
+                        put(v, x, new[v], last)
+
+    def ac_finish(s, last):
         half_dt = 0.15
         UROWS = PAD * 8
 
@@ -429,8 +445,8 @@
 
         vx = [tile(land, s, NB + o) for o in range(2)]
         for o, c in enumerate((1, 2)):
-            ul[uslab(c, -1), :] = jnp.where(tab[5, 0] > 0, vx[o][:8], ul[uslab(c, 0), :])
-            ul[uslab(c, BS), :] = jnp.where(tab[5, 1] > 0, vx[o][8:], ul[uslab(c, BS - 1), :])
+            ul[uslab(c, -1), :] = jnp.where(tab[16, 0] >= 0, vx[o][:8], ul[uslab(c, 0), :])
+            ul[uslab(c, BS), :] = jnp.where(tab[17, 0] >= 0, vx[o][8:], ul[uslab(c, BS - 1), :])
 
         vy = [tile(land, s, NB + 2 + o) for o in range(2)]
         for side, row, alpha in ((0, 0, half_dt), (1, 7, -half_dt)):
@@ -449,7 +465,7 @@
                 terms = side_terms(h, m, 1, alpha)
                 u = [ul[strided(UROWS, c, 8), :] for c in range(3)]
                 hx, hz = [
-                    jnp.where(tab[5, 2 + side] > 0, turned(vy[o][8 * side:8 * side + 8]), u[c])
+                    jnp.where(tab[18 + side, 0] >= 0, turned(vy[o][8 * side:8 * side + 8]), u[c])
                     for o, c in enumerate((0, 2))
                 ]
                 terms[1] = terms[1] + alpha * (u[1] * hx)
@@ -481,8 +497,8 @@
                     got = vz[o][8 * half:8 * half + 8]
                     low = pltpu.roll(got, (97 + amount) % 128, 1)
                     high = pltpu.roll(got, (31 + amount) % 128, 1)
-                    low = jnp.where(tab[5, 4] > 0, low, u[c])
-                    high = jnp.where(tab[5, 5] > 0, high, u[c])
+                    low = jnp.where(tab[20, 0] >= 0, low, u[c])
+                    high = jnp.where(tab[21, 0] >= 0, high, u[c])
                     dz.append(0.5 * (jnp.where(z_high, high, pltpu.roll(u[c], 127, 1))
                                      - jnp.where(z_low, low, pltpu.roll(u[c], 1, 1))))
                 dzu, dzv = dz
@@ -492,7 +508,7 @@
                     val = acc[aslab(v, x), :] + jnp.where(edge, terms[v], 0.0)
                     if 1 <= v <= 3:
                         val = val - 0.3 * lamb[v - 1]
-                    q[slab(v, x), :] = val
+                    put(v, x, val, last)
 
     pack(0)
     pl.semaphore_wait(barrier, NB)
@@ -503,6 +519,13 @@
     def _():
         pltpu.make_async_copy(mean4, mean4, load_sem.at[1]).wait()
 
+    for copy in idx_copies:
+        copy.wait()
+    for i in range(3):
+        idx_v[pl.ds(i, 1), pl.ds(0, NB)] = lists[i][...]
+    for i in range(2):
+        idx_v[pl.ds(8 + 8 * i, 6), pl.ds(0, NB)] = lists[3 + i][...]
+    make_tables()
     for s in range(STEPS):
         if s:
             pack(s)
@@ -518,6 +541,7 @@
 
         if s == 0:
             pl.semaphore_wait(side_sem, 1)
+            pltpu.make_async_copy(tab_v, tab, tab_sem).wait()
         pltpu.make_async_copy(recv_a[s], recv_a[s], ra.at[s]).wait()
         tangential = send_b(s)
         got = land.at[s, pl.ds(0, NB - 1)]
@@ -529,15 +553,8 @@
 
         @pl.when(acoustic)
         def _():
-            ac_finish(s)
-
-    def out_copy(c):
-        return pltpu.make_async_copy(
-            q4.at[:, pl.ds(1, BS), c, :], out_hbm.at[0, 0, :, :, pl.ds(128 * c, 128)], out_sem
-        )
-
-    for c in range(8):
-        out_copy(c).start()
+            ac_finish(s, s == STEPS - 1)
+
     for s in range(STEPS):
         sent = tile_a.at[s, pl.ds(0, NB - 1)]
         pltpu.make_async_copy(sent, sent, sa.at[s]).wait()
@@ -560,18 +577,14 @@
             extra = sort_b.at[s, 1]
             pltpu.make_async_copy(extra, extra, sb.at[STEPS + s]).wait()
 
-    final = q4.at[:, pl.ds(1, BS)]
-    pltpu.make_async_copy(final, final, out_sem).wait()
-
 
 def on_device(state, mean_flow, les_owner, ac_owner, les_nbr, ac_nbr, coupling):
-    tables = make_tables(les_owner, ac_owner, les_nbr, ac_nbr, coupling)
-    hbm = pl.BlockSpec(memory_space=pl.ANY)
-    return pl.pallas_call(
+    hbm = pl.BlockSpec(memory_space=pltpu.HBM)
+    rows = pl.pallas_call(
         kernel,
-        out_shape=jax.ShapeDtypeStruct(state.shape, F32),
-        in_specs=[pl.BlockSpec(memory_space=pltpu.SMEM), hbm, hbm],
-        out_specs=hbm,
+        out_shape=pltpu.VMEM((5 * BS * 8, 128), F32),
+        in_specs=[hbm] * 7,
+        out_specs=pl.BlockSpec(memory_space=pltpu.VMEM),
         scratch_shapes=[
             pltpu.VMEM((5 * ROWS, 128), F32),
             pltpu.VMEM((5 * BS * 8, 128), F32),
@@ -583,20 +596,30 @@
             pltpu.VMEM((STEPS, 2, NB, 16, 128), BF16),
             pltpu.VMEM((STEPS, NB + 6, 16, 128), BF16),
             pltpu.VMEM((16, 128), BF16),
+            pltpu.VMEM((1, NB), jnp.int32),
+            pltpu.VMEM((1, NB), jnp.int32),
+            pltpu.VMEM((1, NB), jnp.int32),
+            pltpu.VMEM((6, NB), jnp.int32),
+            pltpu.VMEM((6, NB), jnp.int32),
+            pltpu.VMEM((24, 128), jnp.int32),
+            pltpu.VMEM((24, 128), jnp.int32),
+            pltpu.SMEM((24, 128), jnp.int32),
+            pltpu.SemaphoreType.DMA((5,)),
             pltpu.SemaphoreType.DMA((2,)),
-            pltpu.SemaphoreType.DMA((1,)),
+            pltpu.SemaphoreType.DMA(()),
             pltpu.SemaphoreType.DMA((STEPS,)),
             pltpu.SemaphoreType.DMA((STEPS,)),
             pltpu.SemaphoreType.DMA((2 * STEPS,)),
             pltpu.SemaphoreType.DMA((STEPS,)),
             pltpu.SemaphoreType.DMA((STEPS,)),
-            pltpu.SemaphoreType.DMA(()),
             pltpu.SemaphoreType.REGULAR,
         ],
         compiler_params=pltpu.CompilerParams(
-            collective_id=0, has_side_effects=True, vmem_limit_bytes=24 << 20
+            collective_id=0, has_side_effects=True, vmem_limit_bytes=60 << 20
         ),
-    )(tables, state, mean_flow)
+    )(les_owner[None], ac_owner[None], coupling[None], les_nbr.T, ac_nbr.T, state, mean_flow)
+    tiles = rows.reshape(5, BS // 8, 8, 8, 128).transpose(0, 1, 3, 2, 4)
+    return tiles.reshape(state.shape)
 
 
 def solution(mesh):

time: 51.9 us -> 40 us (0.77)
  other arithmetic: 7.4 us -> 0 us
  local copies, waits for them, and re-layouts: 3.08 us -> 0.84 us
  Pallas kernels: 41.1 us -> 39 us
    reduce_sum x11 -> x0, other arithmetic: 7.15 us -> none  [the longest x6 4.22 us: lookup(): return jnp.sum(hit * table[None, :], axis=1)]
    pallas_call x1, Pallas kernels: 41.1 us -> 39 us  [on_device(): pl.pallas_call(kernel, out_shape=pltpu.VMEM((5 * BS * 8, 128), F32), in_s...]
    unnamed x5 -> x1, local copies, waits for them, and re-layouts: 1.93 us -> 0.84 us
where the time goes in v2:
time: 40 us; the launch traced here: 39.9 us
  Pallas kernels  39 us (98%)
  local copies, waits for them, and re-layouts  0.84 us (2%)
    pallas_call x1, Pallas kernels, on_device(): pl.pallas_call(kernel, out_shape=pltpu.VMEM((5 * BS * 8, 128), F32), in_s...  39 us
    unnamed x1, local copies, waits for them, and re-layouts  0.84 us

profile of v2, /device:TPU:1, one launch (start us, length us, event | category | flops | bytes accessed | tf_op | source)
XLA Modules:
  0.0 39.9 jit_solution(17857495725795431155)
XLA Ops:
  0.0 39.0 %shard_map.73 = f32[1280,128]{1,0:T(8,128)S(1)} custom-call(s32[1,64]{1,0:T(1,128)} %bitcast.13, s32[1,64]{1,0:T(1,128)} %bitcast.14, s32[1,64]{1,0:T(1,128)} %bitcast.15, s32[6,64]{1,0:T(8,128)} %bitcast.11, s32[6,64]{1,0:T(8,128)} %bitcast.12, f32[1,1,5,32,1024]{4,3,2,1,0:T(8,128)} %state_hbm.1, f32[1,5,32,1024]{3,2,1,0:T(8,128)} %mean_hbm.1), custom_call_target="tpu_custom_call" | custom-call | tf_op jit(solution)/shard_map/pallas_call | solution.py:583
  39.1 0.8 %copy.9 = f32[1,1,5,32,1024]{4,3,2,1,0:T(8,128)} copy(f32[1,1,5,32,1024]{4,3,2,1,0:T(8,128)S(1)} %bitcast.10) | data formatting | bytes 1310720

commit v3 on v2

--- a/solution.py
+++ b/solution.py
@@ -217,24 +217,21 @@
 
         lax.fori_loop(0, 5, faces, 0)
 
+    def others(go, unroll):
+        lax.fori_loop(0, 42, go, 0, unroll=unroll)
+        lax.fori_loop(43, NB, go, 0, unroll=unroll)
+
     def send_a(s):
         def go(n, carry):
             j = partner(n)
-
-            @pl.when(j != me)
-            def _():
-                pltpu.make_async_remote_copy(
-                    src_ref=tile_a.at[s, j], dst_ref=recv_a[s].at[me], send_sem=sa.at[s], recv_sem=ra.at[s],
-                    device_id=(section, j), device_id_type=MESH,
-                ).start()
-
-            @pl.when(j == me)
-            def _():
-                pltpu.make_async_copy(tile_a.at[s, me], recv_a[s].at[me], ra.at[s]).start()
-
-            return carry
-
-        lax.fori_loop(0, NB, go, 0)
+            pltpu.make_async_remote_copy(
+                src_ref=tile_a.at[s, j], dst_ref=recv_a[s].at[me], send_sem=sa.at[s], recv_sem=ra.at[s],
+                device_id=(section, j), device_id_type=MESH,
+            ).start()
+            return carry
+
+        others(go, 1)
+        pltpu.make_async_copy(tile_a.at[s, me], recv_a[s].at[me], ra.at[s]).start()
 
     def put(v, x, value, last):
         if last:
@@ -312,35 +309,50 @@
         vel_slot = NB + jnp.maximum(2 * axis_k + comp - jnp.where(comp > axis_k, 1, 0), 0)
         from_low = pick_ref[...] > 0.5
 
-        @pl.when(me != NB - 1)
-        def _():
-            def go(n, carry):
-                dest = partner(n)
-                sort_b[s, 0, dest] = jnp.where(from_low, recv_a[s][tab[0, dest]], recv_a[s][tab[1, dest]])
-                local = (target == section) & (dest == me)
-
-                @pl.when(jnp.logical_not(local))
-                def _():
-                    pltpu.make_async_remote_copy(
-                        src_ref=sort_b.at[s, 0, dest], dst_ref=land.at[s, me], send_sem=sb.at[s],
-                        recv_sem=rb.at[s], device_id=(target, dest), device_id_type=MESH,
-                    ).start()
-
-                @pl.when(local)
-                def _():
-                    pltpu.make_async_copy(sort_b.at[s, 0, dest], land.at[s, me], rb.at[s]).start()
-
-                @pl.when(tangential)
-                def _():
-                    sort_b[s, 1, dest] = jnp.where(from_low, recv_a[s][tab[2, dest]], recv_a[s][tab[3, dest]])
-                    pltpu.make_async_remote_copy(
-                        src_ref=sort_b.at[s, 1, dest], dst_ref=land.at[s, vel_slot], send_sem=sb.at[STEPS + s],
-                        recv_sem=rv.at[s], device_id=(1, dest), device_id_type=MESH,
-                    ).start()
-
-                return carry
-
-            lax.fori_loop(0, NB, go, 0)
+        def join(slot, dest):
+            low, high = recv_a[s][tab[2 * slot, dest]], recv_a[s][tab[2 * slot + 1, dest]]
+            sort_b[s, slot, dest] = jnp.where(from_low, low, high)
+
+        def send_main(dest):
+            join(0, dest)
+            pltpu.make_async_remote_copy(
+                src_ref=sort_b.at[s, 0, dest], dst_ref=land.at[s, me], send_sem=sb.at[s],
+                recv_sem=rb.at[s], device_id=(target, dest), device_id_type=MESH,
+            ).start()
+
+        def send_vel(dest):
+            join(1, dest)
+            pltpu.make_async_remote_copy(
+                src_ref=sort_b.at[s, 1, dest], dst_ref=land.at[s, vel_slot], send_sem=sb.at[STEPS + s],
+                recv_sem=rv.at[s], device_id=(1, dest), device_id_type=MESH,
+            ).start()
+
+        def go_main(n, carry):
+            send_main(partner(n))
+            return carry
+
+        def go_vel(n, carry):
+            send_vel(partner(n))
+            return carry
+
+        @pl.when((me != NB - 1) & jnp.logical_not(tangential))
+        def _():
+            others(go_main, 1)
+
+            @pl.when(me < NCELL)
+            def _():
+                send_main(me)
+
+        @pl.when(tangential)
+        def _():
+            others(go_vel, 1)
+            send_vel(me)
+            others(go_main, 1)
+
+        @pl.when((me >= NCELL) & (me != NB - 1))
+        def _():
+            join(0, me)
+            pltpu.make_async_copy(sort_b.at[s, 0, me], land.at[s, me], rb.at[s]).start()
 
         return tangential
 

time: 40 us -> 39 us (0.975)
  Pallas kernels: 39 us -> 38 us
    pallas_call x1, Pallas kernels: 39 us -> 38 us  [on_device(): pl.pallas_call(kernel, out_shape=pltpu.VMEM((5 * BS * 8, 128), F32), in_s...]
where the time goes in v3:
time: 39 us; the launch traced here: 38.8 us
  Pallas kernels  38 us (97%)
  local copies, waits for them, and re-layouts  0.84 us (2%)
    pallas_call x1, Pallas kernels, on_device(): pl.pallas_call(kernel, out_shape=pltpu.VMEM((5 * BS * 8, 128), F32), in_s...  38 us
    unnamed x1, local copies, waits for them, and re-layouts  0.84 us

profile of v3, /device:TPU:1, one launch (start us, length us, event | category | flops | bytes accessed | tf_op | source)
XLA Modules:
  0.0 38.8 jit_solution(3406471243157434696)
XLA Ops:
  0.0 38.0 %shard_map.73 = f32[1280,128]{1,0:T(8,128)S(1)} custom-call(s32[1,64]{1,0:T(1,128)} %bitcast.13, s32[1,64]{1,0:T(1,128)} %bitcast.14, s32[1,64]{1,0:T(1,128)} %bitcast.15, s32[6,64]{1,0:T(8,128)} %bitcast.11, s32[6,64]{1,0:T(8,128)} %bitcast.12, f32[1,1,5,32,1024]{4,3,2,1,0:T(8,128)} %state_hbm.1, f32[1,5,32,1024]{3,2,1,0:T(8,128)} %mean_hbm.1), custom_call_target="tpu_custom_call" | custom-call | tf_op jit(solution)/shard_map/pallas_call | solution.py:595
  38.0 0.8 %copy.9 = f32[1,1,5,32,1024]{4,3,2,1,0:T(8,128)} copy(f32[1,1,5,32,1024]{4,3,2,1,0:T(8,128)S(1)} %bitcast.10) | data formatting | bytes 1310720

commit v4 on v3

--- a/solution.py
+++ b/solution.py
@@ -18,6 +18,13 @@
 BF16 = jnp.bfloat16
 
 
+def links(t):
+    return sum((0, 1, 2, 1)[(t >> shift) & 3] for shift in (0, 2, 4))
+
+
+ORDER = sorted((42 ^ n for n in range(NB) if n != 42), key=lambda t: -links(t))
+
+
 def kernel(les_owner, ac_owner, coupling, les_nbr, ac_nbr, state_hbm, mean_hbm, out_ref, q, acc, mean, ul, tile_a, recv_0, recv_1, sort_b, land, pick_ref,
            list_0, list_1, list_2, near_0, near_1, idx_v, tab_v, tab, idx_sem, load_sem, tab_sem, sa, ra, sb, rb, rv, side_sem):
     section = lax.axis_index("section")
@@ -28,19 +35,10 @@
     acc4 = acc.reshape(5, BS, 8, 128)
     mean4 = mean.reshape(5, BS, 8, 128)
 
-    def partner(n):
-        return me ^ (n ^ 42)
-
     barrier = pltpu.get_barrier_semaphore()
 
-    def greet(n, carry):
-        @pl.when(n != 42)
-        def _():
-            pl.semaphore_signal(barrier, inc=1, device_id=(section, partner(n)), device_id_type=MESH)
-
-        return carry
-
-    lax.fori_loop(0, NB, greet, 0)
+    for bits in ORDER:
+        pl.semaphore_signal(barrier, inc=1, device_id=(section, me ^ bits), device_id_type=MESH)
     pl.semaphore_signal(barrier, inc=1, device_id=(1 - section, me), device_id_type=MESH)
 
     recv_a = (recv_0, recv_1)
@@ -217,20 +215,18 @@
 
         lax.fori_loop(0, 5, faces, 0)
 
-    def others(go, unroll):
-        lax.fori_loop(0, 42, go, 0, unroll=unroll)
-        lax.fori_loop(43, NB, go, 0, unroll=unroll)
+    def others(go):
+        for bits in ORDER:
+            go(me ^ bits)
 
     def send_a(s):
-        def go(n, carry):
-            j = partner(n)
+        def go(j):
             pltpu.make_async_remote_copy(
                 src_ref=tile_a.at[s, j], dst_ref=recv_a[s].at[me], send_sem=sa.at[s], recv_sem=ra.at[s],
                 device_id=(section, j), device_id_type=MESH,
             ).start()
-            return carry
-
-        others(go, 1)
+
+        others(go)
         pltpu.make_async_copy(tile_a.at[s, me], recv_a[s].at[me], ra.at[s]).start()
 
     def put(v, x, value, last):
@@ -327,17 +323,9 @@
                 recv_sem=rv.at[s], device_id=(1, dest), device_id_type=MESH,
             ).start()
 
-        def go_main(n, carry):
-            send_main(partner(n))
-            return carry
-
-        def go_vel(n, carry):
-            send_vel(partner(n))
-            return carry
-
         @pl.when((me != NB - 1) & jnp.logical_not(tangential))
         def _():
-            others(go_main, 1)
+            others(send_main)
 
             @pl.when(me < NCELL)
             def _():
@@ -345,9 +333,9 @@
 
         @pl.when(tangential)
         def _():
-            others(go_vel, 1)
+            others(send_vel)
             send_vel(me)
-            others(go_main, 1)
+            others(send_main)
 
         @pl.when((me >= NCELL) & (me != NB - 1))
         def _():

time: 39 us -> 37.8 us (0.969)
  Pallas kernels: 38 us -> 36.8 us
    pallas_call x1, Pallas kernels: 38 us -> 36.8 us  [on_device(): pl.pallas_call(kernel, out_shape=pltpu.VMEM((5 * BS * 8, 128), F32), in_s...]
where the time goes in v4:
time: 37.8 us; the launch traced here: 37.7 us
  Pallas kernels  36.8 us (97%)
  local copies, waits for them, and re-layouts  0.84 us (2%)
    pallas_call x1, Pallas kernels, on_device(): pl.pallas_call(kernel, out_shape=pltpu.VMEM((5 * BS * 8, 128), F32), in_s...  36.8 us
    unnamed x1, local copies, waits for them, and re-layouts  0.84 us

profile of v4, /device:TPU:1, one launch (start us, length us, event | category | flops | bytes accessed | tf_op | source)
XLA Modules:
  0.0 37.7 jit_solution(7934937596585375406)
XLA Ops:
  0.0 36.8 %shard_map.73 = f32[1280,128]{1,0:T(8,128)S(1)} custom-call(s32[1,64]{1,0:T(1,128)} %bitcast.13, s32[1,64]{1,0:T(1,128)} %bitcast.14, s32[1,64]{1,0:T(1,128)} %bitcast.15, s32[6,64]{1,0:T(8,128)} %bitcast.11, s32[6,64]{1,0:T(8,128)} %bitcast.12, f32[1,1,5,32,1024]{4,3,2,1,0:T(8,128)} %state_hbm.1, f32[1,5,32,1024]{3,2,1,0:T(8,128)} %mean_hbm.1), custom_call_target="tpu_custom_call" | custom-call | tf_op jit(solution)/shard_map/pallas_call | solution.py:583
  36.8 0.8 %copy.9 = f32[1,1,5,32,1024]{4,3,2,1,0:T(8,128)} copy(f32[1,1,5,32,1024]{4,3,2,1,0:T(8,128)S(1)} %bitcast.10) | data formatting | bytes 1310720

commit v5 on v4

--- a/solution.py
+++ b/solution.py
@@ -187,7 +187,7 @@
                 tile_a[s, c * 16 + p] = q[pl.ds(start, 16), :].astype(BF16)
             return carry
 
-        lax.fori_loop(0, 16, cells, 0, unroll=4)
+        lax.fori_loop(0, 16, cells, 0, unroll=16)
 
         def faces(v, carry):
             tile_a[s, NCELL + v] = jnp.concatenate(
@@ -213,7 +213,7 @@
             tile_a[s, NCELL + 10 + v] = jnp.concatenate(halves, axis=0).astype(BF16)
             return carry
 
-        lax.fori_loop(0, 5, faces, 0)
+        lax.fori_loop(0, 5, faces, 0, unroll=5)
 
     def others(go):
         for bits in ORDER:
@@ -333,9 +333,11 @@
 
         @pl.when(tangential)
         def _():
-            others(send_vel)
+            for part in (ORDER[:22], ORDER[22:]):
+                for send in (send_vel, send_main):
+                    for bits in part:
+                        send(me ^ bits)
             send_vel(me)
-            others(send_main)
 
         @pl.when((me >= NCELL) & (me != NB - 1))
         def _():
@@ -419,7 +421,7 @@
                 ul[pl.ds(pl.multiple_of(c * UROWS + 16 * p + 8, 8), 16), :] = tile(land, s, c * 16 + p)
             return carry
 
-        lax.fori_loop(0, 16, unpack, 0, unroll=4)
+        lax.fori_loop(0, 16, unpack, 0, unroll=16)
 
         pairs = [halo_rows(s, 0, v) for v in range(5)]
 
@@ -475,7 +477,13 @@
                     where = strided(BS * 8, v, 0)
                     acc[where, :] = acc[where, :] + jnp.where(keep, terms[v], 0.0)
 
-        vz = [tile(land, s, NB + 4 + o) for o in range(2)]
+        vz = []
+        for o in range(2):
+            got = tile(land, s, NB + 4 + o)
+            vz.append([
+                jnp.where(even, pltpu.roll(got[8 * h:8 * h + 8], 97, 1), pltpu.roll(got[8 * h:8 * h + 8], 31, 1))
+                for h in range(2)
+            ])
         edge = z_low | z_high
         alpha_z = jnp.where(z_low, half_dt, -half_dt)
         for half in range(2):
@@ -494,11 +502,9 @@
                 dyu, dyw = [0.5 * (up_y(u[c]) - dn_y(u[c])) for c in (0, 2)]
                 dz = []
                 for o, c in enumerate((0, 1)):
-                    got = vz[o][8 * half:8 * half + 8]
-                    low = pltpu.roll(got, (97 + amount) % 128, 1)
-                    high = pltpu.roll(got, (31 + amount) % 128, 1)
-                    low = jnp.where(tab[20, 0] >= 0, low, u[c])
-                    high = jnp.where(tab[21, 0] >= 0, high, u[c])
+                    got = turned(vz[o][half])
+                    low = jnp.where(tab[20, 0] >= 0, got, u[c])
+                    high = jnp.where(tab[21, 0] >= 0, got, u[c])
                     dz.append(0.5 * (jnp.where(z_high, high, pltpu.roll(u[c], 127, 1))
                                      - jnp.where(z_low, low, pltpu.roll(u[c], 1, 1))))
                 dzu, dzv = dz

time: 37.8 us -> 37.3 us (0.987)
  Pallas kernels: 36.8 us -> 36.3 us
    pallas_call x1, Pallas kernels: 36.8 us -> 36.3 us  [on_device(): pl.pallas_call(kernel, out_shape=pltpu.VMEM((5 * BS * 8, 128), F32), in_s...]
where the time goes in v5:
time: 37.3 us; the launch traced here: 37.1 us
  Pallas kernels  36.3 us (97%)
  local copies, waits for them, and re-layouts  0.84 us (2%)
    pallas_call x1, Pallas kernels, on_device(): pl.pallas_call(kernel, out_shape=pltpu.VMEM((5 * BS * 8, 128), F32), in_s...  36.3 us
    unnamed x1, local copies, waits for them, and re-layouts  0.84 us

profile of v5, /device:TPU:1, one launch (start us, length us, event | category | flops | bytes accessed | tf_op | source)
XLA Modules:
  0.0 37.1 jit_solution(12140592140798787844)
XLA Ops:
  0.0 36.3 %shard_map.73 = f32[1280,128]{1,0:T(8,128)S(1)} custom-call(s32[1,64]{1,0:T(1,128)} %bitcast.13, s32[1,64]{1,0:T(1,128)} %bitcast.14, s32[1,64]{1,0:T(1,128)} %bitcast.15, s32[6,64]{1,0:T(8,128)} %bitcast.11, s32[6,64]{1,0:T(8,128)} %bitcast.12, f32[1,1,5,32,1024]{4,3,2,1,0:T(8,128)} %state_hbm.1, f32[1,5,32,1024]{3,2,1,0:T(8,128)} %mean_hbm.1), custom_call_target="tpu_custom_call" | custom-call | tf_op jit(solution)/shard_map/pallas_call | solution.py:589
  36.3 0.8 %copy.9 = f32[1,1,5,32,1024]{4,3,2,1,0:T(8,128)} copy(f32[1,1,5,32,1024]{4,3,2,1,0:T(8,128)S(1)} %bitcast.10) | data formatting | bytes 1310720
